TPU v7x, 512 devices: a whole 4x4x16 slice. The times are simulated.
512 devices in a mesh: section: 4 (over y), tm: 4 (over x_lo, core), space: 32 (over z, x_hi).
Axes of the slice: x: 4 (x_hi: 2, x_lo: 2; x = x_hi * 2 + x_lo), y: 4, z: 16, core: 2. Of those that a mesh axis runs over, the one named last changes fastest.
Arguments:
- clip_features: bfloat16 [8, 64, 64, 256], P('tm', 'space'), may hold values from -6 to 6
- conv_kernels: bfloat16 [4, 9, 768, 256], P('section'), may hold values from -0.078125 to 0.078125
- norm_gains: float32 [4, 256], P('section'), may hold values from 0.1 to 1.9
Outputs:
- section_outputs: bfloat16 [4, 8, 64, 64, 256], P('section', 'tm', 'space')
All inputs are finite; a program needn't handle non-finite values.
Results may differ from a plain program's by a relative error of at most 0.018.
Values may be sent and summed in bfloat16 or wider, within the bound.
A program may use at most 64 MiB of HBM per device.

v0:
```python
import jax
import jax.numpy as jnp
from jax import lax
from jax.sharding import PartitionSpec as P


def passed_along(block, axis, distance):
    devices = range(lax.axis_size(axis))
    route = [(i - distance, i) for i in devices if i - distance in devices]
    return lax.ppermute(block, axis, route)


def padded_2(cells, sides, width):
    for axis, dim in sides:
        count = lax.axis_size(axis)
        ends = count - 1
        head = lax.slice_in_dim(cells, 0, width, axis=dim)
        tail = lax.slice_in_dim(cells, cells.shape[dim] - width, cells.shape[dim], axis=dim)
        cells = jnp.concatenate(
            [
                lax.ppermute(tail, axis, [(i, (i + 1) % count) for i in range(ends)]),
                cells,
                lax.ppermute(head, axis, [((i + 1) % count, i) for i in range(ends)]),
            ],
            axis=dim,
        )
    return cells


def normed(inputs, norm_gain):
    wide = inputs.astype(jnp.float32)
    factor = lax.rsqrt(jnp.mean(wide * wide, axis=-1, keepdims=True) + 1e-06)
    return jax.nn.silu(wide * factor * norm_gain).astype(jnp.bfloat16)


def with_cache(hidden):
    carried = passed_along(hidden, "tm", 1)
    return jnp.concatenate([carried, hidden], axis=0)


def convolve(padded, kernel):
    frame_count = padded.shape[0] - 2
    row_count = padded.shape[1] - 2
    col_count = padded.shape[2] - 2
    channels = padded.shape[3]
    summed = jnp.zeros((frame_count * row_count * col_count, channels), jnp.float32)
    for time_tap in range(3):
        for row_tap in range(3):
            window = padded[time_tap : time_tap + frame_count, row_tap : row_tap + row_count]
            stacked = jnp.concatenate(
                [
                    window[:, :, 0:col_count],
                    window[:, :, 1 : col_count + 1],
                    window[:, :, 2 : col_count + 2],
                ],
                axis=-1,
            )
            summed = summed + jnp.dot(
                stacked.reshape(-1, 3 * channels),
                kernel[3 * time_tap + row_tap],
                preferred_element_type=jnp.float32,
            )
    return summed.reshape(frame_count, row_count, col_count, channels)


def on_device(clip_features, conv_kernels, norm_gains):
    section_at = lax.axis_index("section")
    n_sections = lax.axis_size("section")
    kernel = conv_kernels[0]
    gains = norm_gains[0]
    current = clip_features
    kept = jnp.zeros_like(current)

    def apply_layer(inputs, padded):
        return (inputs.astype(jnp.float32) + convolve(padded, kernel)).astype(jnp.bfloat16)

    def skip_layer(inputs, padded):
        return jnp.zeros_like(inputs)

    for tick in range(n_sections):
        hidden = normed(current, gains)
        cached = with_cache(hidden)
        padded = padded_2(cached, (("space", 1),), 1)
        padded = jnp.pad(padded, ((0, 0), (0, 0), (1, 1), (0, 0)))
        result = lax.cond(section_at == tick, apply_layer, skip_layer, current, padded)
        kept = jnp.where(section_at == tick, result, kept)
        if tick + 1 < n_sections:
            current = passed_along(result, "section", 1)
    return kept[None]


def solution(mesh):
    return jax.shard_map(
        on_device,
        mesh=mesh,
        in_specs=(P("tm", "space", None, None), P("section", None, None, None), P("section", None)),
        out_specs=P("section", "tm", "space", None, None),
        check_vma=False,
    )
```

profile of v0, /device:TPU:222, one launch (start us, length us, event | category | flops | bytes accessed | tf_op | source)
XLA Modules:
  0.0 122.4 jit_solution(11051448960401547490)
XLA Ops:
  0.0 1.0 fusion.76
  1.0 1.1 fusion.83
  2.1 1.9 %collective-permute-start = (bf16[2,2,64,256]{3,2,1,0:T(8,128)(2,1)S(1)}, bf16[2,2,64,256]{3,2,1,0:T(8,128)(2,1)S(1)}, u32[]{:S(2)}, u32[]{:S(2)}) collective-permute-start(bf16[2,2,64,256]{3,2,1,0:T(8,128)(2,1)S(1)} %fusion.83), channel_id=1, source_target_pairs={{0,32},{32,64},{64,96},{1,33},{33,65},{65,97},{2,34},{34,66},{66,9... | collective-permute-start | bytes 393224 | tf_op jit(solution)/shard_map/ppermute | solution.py:10
  4.0 4.4 %collective-permute-done = bf16[2,2,64,256]{3,2,1,0:T(8,128)(2,1)S(1)} collective-permute-done((bf16[2,2,64,256]{3,2,1,0:T(8,128)(2,1)S(1)}, bf16[2,2,64,256]{3,2,1,0:T(8,128)(2,1)S(1)}, u32[]{:S(2)}, u32[]{:S(2)}) %collective-permute-start) | collective-permute-done | bytes 131104 | tf_op jit(solution)/shard_map/ppermute | solution.py:10
  8.4 4.7 %collective-permute-start.1 = (bf16[4,1,64,256]{3,2,1,0:T(8,128)(2,1)S(1)}, bf16[4,1,64,256]{3,2,1,0:T(8,128)(2,1)S(1)}, u32[]{:S(2)}, u32[]{:S(2)}) collective-permute-start(bf16[4,1,64,256]{3,2,1,0:T(8,128)(2,1)S(1)} %get-tuple-element.207), channel_id=1, source_target_pairs={{0,1},{1,2},{2,3},{3,4},{4,5},{5,6},{6,7},{7,8},{8,9},{9,10},{10,1... | collective-permute-start | bytes 393224 | tf_op jit(solution)/shard_map/ppermute | solution.py:21
  13.1 2.7 %collective-permute-start.2 = (bf16[4,1,64,256]{3,2,1,0:T(8,128)(2,1)S(1)}, bf16[4,1,64,256]{3,2,1,0:T(8,128)(2,1)S(1)}, u32[]{:S(2)}, u32[]{:S(2)}) collective-permute-start(bf16[4,1,64,256]{3,2,1,0:T(8,128)(2,1)S(1)} %get-tuple-element.208), channel_id=1, source_target_pairs={{1,0},{2,1},{3,2},{4,3},{5,4},{6,5},{7,6},{8,7},{9,8},{10,9},{11,1... | collective-permute-start | bytes 393224 | tf_op jit(solution)/shard_map/ppermute | solution.py:23
  15.8 2.4 %collective-permute-done.1 = bf16[4,1,64,256]{3,2,1,0:T(8,128)(2,1)S(1)} collective-permute-done((bf16[4,1,64,256]{3,2,1,0:T(8,128)(2,1)S(1)}, bf16[4,1,64,256]{3,2,1,0:T(8,128)(2,1)S(1)}, u32[]{:S(2)}, u32[]{:S(2)}) %collective-permute-start.1) | collective-permute-done | bytes 131104 | tf_op jit(solution)/shard_map/ppermute | solution.py:21
  18.2 4.2 %collective-permute-done.2 = bf16[4,1,64,256]{3,2,1,0:T(8,128)(2,1)S(1)} collective-permute-done((bf16[4,1,64,256]{3,2,1,0:T(8,128)(2,1)S(1)}, bf16[4,1,64,256]{3,2,1,0:T(8,128)(2,1)S(1)}, u32[]{:S(2)}, u32[]{:S(2)}) %collective-permute-start.2) | collective-permute-done | bytes 131104 | tf_op jit(solution)/shard_map/ppermute | solution.py:23
  22.4 0.1 pad_maximum_fusion.36
  22.4 0.0 copy-start.5
  22.5 1.3 %collective-permute-start.3 = (bf16[2,2,64,256]{3,2,1,0:T(8,128)(2,1)S(1)}, bf16[2,2,64,256]{3,2,1,0:T(8,128)(2,1)S(1)}, u32[]{:S(2)}, u32[]{:S(2)}) collective-permute-start(bf16[2,2,64,256]{3,2,1,0:T(8,128)(2,1)S(1)} %get-tuple-element.209), channel_id=1, source_target_pairs={{0,128},{128,256},{256,384},{1,129},{129,257},{257,385},{2,130},{1... | collective-permute-start | bytes 393224 | tf_op jit(solution)/shard_map/ppermute | solution.py:10
  23.8 5.6 %collective-permute-done.3 = bf16[2,2,64,256]{3,2,1,0:T(8,128)(2,1)S(1)} collective-permute-done((bf16[2,2,64,256]{3,2,1,0:T(8,128)(2,1)S(1)}, bf16[2,2,64,256]{3,2,1,0:T(8,128)(2,1)S(1)}, u32[]{:S(2)}, u32[]{:S(2)}) %collective-permute-start.3) | collective-permute-done | bytes 131104 | tf_op jit(solution)/shard_map/ppermute | solution.py:10
  29.3 0.1 fusion.84
  29.5 0.0 copy-done.5
  29.5 0.1 fusion.91
  29.6 1.9 %collective-permute-start.4 = (bf16[2,2,64,256]{3,2,1,0:T(8,128)(2,1)S(1)}, bf16[2,2,64,256]{3,2,1,0:T(8,128)(2,1)S(1)}, u32[]{:S(2)}, u32[]{:S(2)}) collective-permute-start(bf16[2,2,64,256]{3,2,1,0:T(8,128)(2,1)S(1)} %fusion.91), channel_id=1, source_target_pairs={{0,32},{32,64},{64,96},{1,33},{33,65},{65,97},{2,34},{34,66},{66,9... | collective-permute-start | bytes 393224 | tf_op jit(solution)/shard_map/ppermute | solution.py:10
  31.6 5.8 %collective-permute-done.4 = bf16[2,2,64,256]{3,2,1,0:T(8,128)(2,1)S(1)} collective-permute-done((bf16[2,2,64,256]{3,2,1,0:T(8,128)(2,1)S(1)}, bf16[2,2,64,256]{3,2,1,0:T(8,128)(2,1)S(1)}, u32[]{:S(2)}, u32[]{:S(2)}) %collective-permute-start.4) | collective-permute-done | bytes 131104 | tf_op jit(solution)/shard_map/ppermute | solution.py:10
  37.4 2.2 %collective-permute-start.5 = (bf16[4,1,64,256]{3,2,1,0:T(8,128)(2,1)S(1)}, bf16[4,1,64,256]{3,2,1,0:T(8,128)(2,1)S(1)}, u32[]{:S(2)}, u32[]{:S(2)}) collective-permute-start(bf16[4,1,64,256]{3,2,1,0:T(8,128)(2,1)S(1)} %get-tuple-element.205), channel_id=1, source_target_pairs={{0,1},{1,2},{2,3},{3,4},{4,5},{5,6},{6,7},{7,8},{8,9},{9,10},{10,1... | collective-permute-start | bytes 393224 | tf_op jit(solution)/shard_map/ppermute | solution.py:21
  39.5 5.2 %collective-permute-start.6 = (bf16[4,1,64,256]{3,2,1,0:T(8,128)(2,1)S(1)}, bf16[4,1,64,256]{3,2,1,0:T(8,128)(2,1)S(1)}, u32[]{:S(2)}, u32[]{:S(2)}) collective-permute-start(bf16[4,1,64,256]{3,2,1,0:T(8,128)(2,1)S(1)} %get-tuple-element.206), channel_id=1, source_target_pairs={{1,0},{2,1},{3,2},{4,3},{5,4},{6,5},{7,6},{8,7},{9,8},{10,9},{11,1... | collective-permute-start | bytes 393224 | tf_op jit(solution)/shard_map/ppermute | solution.py:23
  44.7 2.4 %collective-permute-done.5 = bf16[4,1,64,256]{3,2,1,0:T(8,128)(2,1)S(1)} collective-permute-done((bf16[4,1,64,256]{3,2,1,0:T(8,128)(2,1)S(1)}, bf16[4,1,64,256]{3,2,1,0:T(8,128)(2,1)S(1)}, u32[]{:S(2)}, u32[]{:S(2)}) %collective-permute-start.5) | collective-permute-done | bytes 131104 | tf_op jit(solution)/shard_map/ppermute | solution.py:21
  47.1 2.9 %collective-permute-done.6 = bf16[4,1,64,256]{3,2,1,0:T(8,128)(2,1)S(1)} collective-permute-done((bf16[4,1,64,256]{3,2,1,0:T(8,128)(2,1)S(1)}, bf16[4,1,64,256]{3,2,1,0:T(8,128)(2,1)S(1)}, u32[]{:S(2)}, u32[]{:S(2)}) %collective-permute-start.6) | collective-permute-done | bytes 131104 | tf_op jit(solution)/shard_map/ppermute | solution.py:23
  50.0 0.1 pad_maximum_fusion.37
  50.1 1.3 %collective-permute-start.7 = (bf16[2,2,64,256]{3,2,1,0:T(8,128)(2,1)S(1)}, bf16[2,2,64,256]{3,2,1,0:T(8,128)(2,1)S(1)}, u32[]{:S(2)}, u32[]{:S(2)}) collective-permute-start(bf16[2,2,64,256]{3,2,1,0:T(8,128)(2,1)S(1)} %get-tuple-element.210), channel_id=1, source_target_pairs={{0,128},{128,256},{256,384},{1,129},{129,257},{257,385},{2,130},{1... | collective-permute-start | bytes 393224 | tf_op jit(solution)/shard_map/ppermute | solution.py:10
  51.4 5.6 %collective-permute-done.7 = bf16[2,2,64,256]{3,2,1,0:T(8,128)(2,1)S(1)} collective-permute-done((bf16[2,2,64,256]{3,2,1,0:T(8,128)(2,1)S(1)}, bf16[2,2,64,256]{3,2,1,0:T(8,128)(2,1)S(1)}, u32[]{:S(2)}, u32[]{:S(2)}) %collective-permute-start.7) | collective-permute-done | bytes 131104 | tf_op jit(solution)/shard_map/ppermute | solution.py:10
  57.0 0.1 fusion.92
  57.1 0.2 fusion.99
  57.3 1.9 %collective-permute-start.8 = (bf16[2,2,64,256]{3,2,1,0:T(8,128)(2,1)S(1)}, bf16[2,2,64,256]{3,2,1,0:T(8,128)(2,1)S(1)}, u32[]{:S(2)}, u32[]{:S(2)}) collective-permute-start(bf16[2,2,64,256]{3,2,1,0:T(8,128)(2,1)S(1)} %fusion.99), channel_id=1, source_target_pairs={{0,32},{32,64},{64,96},{1,33},{33,65},{65,97},{2,34},{34,66},{66,9... | collective-permute-start | bytes 393224 | tf_op jit(solution)/shard_map/ppermute | solution.py:10
  59.2 5.0 %collective-permute-done.8 = bf16[2,2,64,256]{3,2,1,0:T(8,128)(2,1)S(1)} collective-permute-done((bf16[2,2,64,256]{3,2,1,0:T(8,128)(2,1)S(1)}, bf16[2,2,64,256]{3,2,1,0:T(8,128)(2,1)S(1)}, u32[]{:S(2)}, u32[]{:S(2)}) %collective-permute-start.8) | collective-permute-done | bytes 131104 | tf_op jit(solution)/shard_map/ppermute | solution.py:10
  64.2 4.8 %collective-permute-start.9 = (bf16[4,1,64,256]{3,2,1,0:T(8,128)(2,1)S(1)}, bf16[4,1,64,256]{3,2,1,0:T(8,128)(2,1)S(1)}, u32[]{:S(2)}, u32[]{:S(2)}) collective-permute-start(bf16[4,1,64,256]{3,2,1,0:T(8,128)(2,1)S(1)} %get-tuple-element.203), channel_id=1, source_target_pairs={{0,1},{1,2},{2,3},{3,4},{4,5},{5,6},{6,7},{7,8},{8,9},{9,10},{10,1... | collective-permute-start | bytes 393224 | tf_op jit(solution)/shard_map/ppermute | solution.py:21
  69.0 2.5 %collective-permute-start.10 = (bf16[4,1,64,256]{3,2,1,0:T(8,128)(2,1)S(1)}, bf16[4,1,64,256]{3,2,1,0:T(8,128)(2,1)S(1)}, u32[]{:S(2)}, u32[]{:S(2)}) collective-permute-start(bf16[4,1,64,256]{3,2,1,0:T(8,128)(2,1)S(1)} %get-tuple-element.204), channel_id=1, source_target_pairs={{1,0},{2,1},{3,2},{4,3},{5,4},{6,5},{7,6},{8,7},{9,8},{10,9},{11,1... | collective-permute-start | bytes 393224 | tf_op jit(solution)/shard_map/ppermute | solution.py:23
  71.6 1.0 collective-permute-done.9
  72.6 5.7 %collective-permute-done.10 = bf16[4,1,64,256]{3,2,1,0:T(8,128)(2,1)S(1)} collective-permute-done((bf16[4,1,64,256]{3,2,1,0:T(8,128)(2,1)S(1)}, bf16[4,1,64,256]{3,2,1,0:T(8,128)(2,1)S(1)}, u32[]{:S(2)}, u32[]{:S(2)}) %collective-permute-start.10) | collective-permute-done | bytes 131104 | tf_op jit(solution)/shard_map/ppermute | solution.py:23
  78.3 0.1 pad_maximum_fusion.38
  78.4 1.3 %collective-permute-start.11 = (bf16[2,2,64,256]{3,2,1,0:T(8,128)(2,1)S(1)}, bf16[2,2,64,256]{3,2,1,0:T(8,128)(2,1)S(1)}, u32[]{:S(2)}, u32[]{:S(2)}) collective-permute-start(bf16[2,2,64,256]{3,2,1,0:T(8,128)(2,1)S(1)} %get-tuple-element.211), channel_id=1, source_target_pairs={{0,128},{128,256},{256,384},{1,129},{129,257},{257,385},{2,130},{1... | collective-permute-start | bytes 393224 | tf_op jit(solution)/shard_map/ppermute | solution.py:10
  79.7 15.5 %collective-permute-done.11 = bf16[2,2,64,256]{3,2,1,0:T(8,128)(2,1)S(1)} collective-permute-done((bf16[2,2,64,256]{3,2,1,0:T(8,128)(2,1)S(1)}, bf16[2,2,64,256]{3,2,1,0:T(8,128)(2,1)S(1)}, u32[]{:S(2)}, u32[]{:S(2)}) %collective-permute-start.11) | collective-permute-done | bytes 131104 | tf_op jit(solution)/shard_map/ppermute | solution.py:10
  95.2 0.1 fusion.100
  95.3 0.2 fusion.107
  95.5 1.9 %collective-permute-start.12 = (bf16[2,2,64,256]{3,2,1,0:T(8,128)(2,1)S(1)}, bf16[2,2,64,256]{3,2,1,0:T(8,128)(2,1)S(1)}, u32[]{:S(2)}, u32[]{:S(2)}) collective-permute-start(bf16[2,2,64,256]{3,2,1,0:T(8,128)(2,1)S(1)} %fusion.107), channel_id=1, source_target_pairs={{0,32},{32,64},{64,96},{1,33},{33,65},{65,97},{2,34},{34,66},{66,9... | collective-permute-start | bytes 393224 | tf_op jit(solution)/shard_map/ppermute | solution.py:10
  97.4 5.8 %collective-permute-done.12 = bf16[2,2,64,256]{3,2,1,0:T(8,128)(2,1)S(1)} collective-permute-done((bf16[2,2,64,256]{3,2,1,0:T(8,128)(2,1)S(1)}, bf16[2,2,64,256]{3,2,1,0:T(8,128)(2,1)S(1)}, u32[]{:S(2)}, u32[]{:S(2)}) %collective-permute-start.12) | collective-permute-done | bytes 131104 | tf_op jit(solution)/shard_map/ppermute | solution.py:10
  103.2 4.0 %collective-permute-start.13 = (bf16[4,1,64,256]{3,2,1,0:T(8,128)(2,1)S(1)}, bf16[4,1,64,256]{3,2,1,0:T(8,128)(2,1)S(1)}, u32[]{:S(2)}, u32[]{:S(2)}) collective-permute-start(bf16[4,1,64,256]{3,2,1,0:T(8,128)(2,1)S(1)} %get-tuple-element.201), channel_id=1, source_target_pairs={{0,1},{1,2},{2,3},{3,4},{4,5},{5,6},{6,7},{7,8},{8,9},{9,10},{10,1... | collective-permute-start | bytes 393224 | tf_op jit(solution)/shard_map/ppermute | solution.py:21
  107.2 3.4 %collective-permute-start.14 = (bf16[4,1,64,256]{3,2,1,0:T(8,128)(2,1)S(1)}, bf16[4,1,64,256]{3,2,1,0:T(8,128)(2,1)S(1)}, u32[]{:S(2)}, u32[]{:S(2)}) collective-permute-start(bf16[4,1,64,256]{3,2,1,0:T(8,128)(2,1)S(1)} %get-tuple-element.202), channel_id=1, source_target_pairs={{1,0},{2,1},{3,2},{4,3},{5,4},{6,5},{7,6},{8,7},{9,8},{10,9},{11,1... | collective-permute-start | bytes 393224 | tf_op jit(solution)/shard_map/ppermute | solution.py:23
  110.6 2.2 %collective-permute-done.13 = bf16[4,1,64,256]{3,2,1,0:T(8,128)(2,1)S(1)} collective-permute-done((bf16[4,1,64,256]{3,2,1,0:T(8,128)(2,1)S(1)}, bf16[4,1,64,256]{3,2,1,0:T(8,128)(2,1)S(1)}, u32[]{:S(2)}, u32[]{:S(2)}) %collective-permute-start.13) | collective-permute-done | bytes 131104 | tf_op jit(solution)/shard_map/ppermute | solution.py:21
  112.7 3.7 %collective-permute-done.14 = bf16[4,1,64,256]{3,2,1,0:T(8,128)(2,1)S(1)} collective-permute-done((bf16[4,1,64,256]{3,2,1,0:T(8,128)(2,1)S(1)}, bf16[4,1,64,256]{3,2,1,0:T(8,128)(2,1)S(1)}, u32[]{:S(2)}, u32[]{:S(2)}) %collective-permute-start.14) | collective-permute-done | bytes 131104 | tf_op jit(solution)/shard_map/ppermute | solution.py:23
  116.5 0.1 pad_maximum_fusion.39
  116.6 5.2 %conditional.7 = (bf16[2,2,64,256]{3,2,1,0:T(8,128)(2,1)S(1)}) conditional(s32[]{:T(128)} %convert_element_type.65, () %tuple.29, (bf16[2,2,64,256]{3,2,1,0:T(8,128)(2,1)S(1)}, bf16[4,4,64,256]{3,2,1,0:T(8,128)(2,1)S(1)}, bf16[9,768,256]{2,1,0:T(8,128)(2,1)}) %tuple.164), branch_computations={%region_10.11_spmd, %region_11.12_spmd} | conditional | flops 917307392 | bytes 39583780 | solution.py:85
  116.8 0.0 copy-start.3
  116.8 0.1 fusion.115
  116.9 0.2 pad_slice_fusion.55
  117.1 0.1 pad_maximum_fusion.27
  117.2 1.6 %copy-done.3 = bf16[9,768,256]{2,1,0:T(8,128)(2,1)S(1)} copy-done((bf16[9,768,256]{2,1,0:T(8,128)(2,1)S(1)}, bf16[9,768,256]{2,1,0:T(8,128)(2,1)}, u32[]{:S(2)}) %copy-start.3) | copy-done | bytes 3538968 | tf_op jit(solution)/shard_map/cond
  118.8 0.3 fusion.65
  119.0 0.3 convolution_add_fusion.31
  119.3 0.1 pad_maximum_fusion.29
  119.4 0.3 convolution_add_fusion.30
  119.7 0.3 convolution_add_fusion.29
  119.9 0.2 pad_slice_fusion.54
  120.2 0.1 pad_maximum_fusion.31
  120.2 0.3 convolution_add_fusion.28
  120.6 0.1 pad_maximum_fusion.32
  120.6 0.3 convolution_add_fusion.27
  120.9 0.3 convolution_add_fusion.26
  121.2 0.3 convolution_add_fusion.25
  121.4 0.3 convolution_add_fusion.24
  121.8 0.7 select_bitcast_fusion
  (16 shorter events, 0.3 us)
Async XLA Ops:
  2.1 6.3 %collective-permute-start = (bf16[2,2,64,256]{3,2,1,0:T(8,128)(2,1)S(1)}, bf16[2,2,64,256]{3,2,1,0:T(8,128)(2,1)S(1)}, u32[]{:S(2)}, u32[]{:S(2)}) collective-permute-start(bf16[2,2,64,256]{3,2,1,0:T(8,128)(2,1)S(1)} %fusion.83), channel_id=1, source_target_pairs={{0,32},{32,64},{64,96},{1,33},{33,65},{65,97},{2,34},{34,66},{66,9... | collective-permute-start | bytes 393224 | tf_op jit(solution)/shard_map/ppermute | solution.py:10
  8.4 9.8 %collective-permute-start.1 = (bf16[4,1,64,256]{3,2,1,0:T(8,128)(2,1)S(1)}, bf16[4,1,64,256]{3,2,1,0:T(8,128)(2,1)S(1)}, u32[]{:S(2)}, u32[]{:S(2)}) collective-permute-start(bf16[4,1,64,256]{3,2,1,0:T(8,128)(2,1)S(1)} %get-tuple-element.207), channel_id=1, source_target_pairs={{0,1},{1,2},{2,3},{3,4},{4,5},{5,6},{6,7},{7,8},{8,9},{9,10},{10,1... | collective-permute-start | bytes 393224 | tf_op jit(solution)/shard_map/ppermute | solution.py:21
  13.1 9.3 %collective-permute-start.2 = (bf16[4,1,64,256]{3,2,1,0:T(8,128)(2,1)S(1)}, bf16[4,1,64,256]{3,2,1,0:T(8,128)(2,1)S(1)}, u32[]{:S(2)}, u32[]{:S(2)}) collective-permute-start(bf16[4,1,64,256]{3,2,1,0:T(8,128)(2,1)S(1)} %get-tuple-element.208), channel_id=1, source_target_pairs={{1,0},{2,1},{3,2},{4,3},{5,4},{6,5},{7,6},{8,7},{9,8},{10,9},{11,1... | collective-permute-start | bytes 393224 | tf_op jit(solution)/shard_map/ppermute | solution.py:23
  22.4 7.1 %copy-start.5 = (f32[1,256]{1,0:T(1,128)S(1)}, f32[1,256]{1,0:T(1,128)}, u32[]{:S(2)}) copy-start(f32[1,256]{1,0:T(1,128)} %param.13) | copy-start | bytes 3076
  22.5 6.9 %collective-permute-start.3 = (bf16[2,2,64,256]{3,2,1,0:T(8,128)(2,1)S(1)}, bf16[2,2,64,256]{3,2,1,0:T(8,128)(2,1)S(1)}, u32[]{:S(2)}, u32[]{:S(2)}) collective-permute-start(bf16[2,2,64,256]{3,2,1,0:T(8,128)(2,1)S(1)} %get-tuple-element.209), channel_id=1, source_target_pairs={{0,128},{128,256},{256,384},{1,129},{129,257},{257,385},{2,130},{1... | collective-permute-start | bytes 393224 | tf_op jit(solution)/shard_map/ppermute | solution.py:10
  29.6 7.7 %collective-permute-start.4 = (bf16[2,2,64,256]{3,2,1,0:T(8,128)(2,1)S(1)}, bf16[2,2,64,256]{3,2,1,0:T(8,128)(2,1)S(1)}, u32[]{:S(2)}, u32[]{:S(2)}) collective-permute-start(bf16[2,2,64,256]{3,2,1,0:T(8,128)(2,1)S(1)} %fusion.91), channel_id=1, source_target_pairs={{0,32},{32,64},{64,96},{1,33},{33,65},{65,97},{2,34},{34,66},{66,9... | collective-permute-start | bytes 393224 | tf_op jit(solution)/shard_map/ppermute | solution.py:10
  37.4 9.8 %collective-permute-start.5 = (bf16[4,1,64,256]{3,2,1,0:T(8,128)(2,1)S(1)}, bf16[4,1,64,256]{3,2,1,0:T(8,128)(2,1)S(1)}, u32[]{:S(2)}, u32[]{:S(2)}) collective-permute-start(bf16[4,1,64,256]{3,2,1,0:T(8,128)(2,1)S(1)} %get-tuple-element.205), channel_id=1, source_target_pairs={{0,1},{1,2},{2,3},{3,4},{4,5},{5,6},{6,7},{7,8},{8,9},{9,10},{10,1... | collective-permute-start | bytes 393224 | tf_op jit(solution)/shard_map/ppermute | solution.py:21
  39.5 10.5 %collective-permute-start.6 = (bf16[4,1,64,256]{3,2,1,0:T(8,128)(2,1)S(1)}, bf16[4,1,64,256]{3,2,1,0:T(8,128)(2,1)S(1)}, u32[]{:S(2)}, u32[]{:S(2)}) collective-permute-start(bf16[4,1,64,256]{3,2,1,0:T(8,128)(2,1)S(1)} %get-tuple-element.206), channel_id=1, source_target_pairs={{1,0},{2,1},{3,2},{4,3},{5,4},{6,5},{7,6},{8,7},{9,8},{10,9},{11,1... | collective-permute-start | bytes 393224 | tf_op jit(solution)/shard_map/ppermute | solution.py:23
  50.1 6.9 %collective-permute-start.7 = (bf16[2,2,64,256]{3,2,1,0:T(8,128)(2,1)S(1)}, bf16[2,2,64,256]{3,2,1,0:T(8,128)(2,1)S(1)}, u32[]{:S(2)}, u32[]{:S(2)}) collective-permute-start(bf16[2,2,64,256]{3,2,1,0:T(8,128)(2,1)S(1)} %get-tuple-element.210), channel_id=1, source_target_pairs={{0,128},{128,256},{256,384},{1,129},{129,257},{257,385},{2,130},{1... | collective-permute-start | bytes 393224 | tf_op jit(solution)/shard_map/ppermute | solution.py:10
  57.3 6.9 %collective-permute-start.8 = (bf16[2,2,64,256]{3,2,1,0:T(8,128)(2,1)S(1)}, bf16[2,2,64,256]{3,2,1,0:T(8,128)(2,1)S(1)}, u32[]{:S(2)}, u32[]{:S(2)}) collective-permute-start(bf16[2,2,64,256]{3,2,1,0:T(8,128)(2,1)S(1)} %fusion.99), channel_id=1, source_target_pairs={{0,32},{32,64},{64,96},{1,33},{33,65},{65,97},{2,34},{34,66},{66,9... | collective-permute-start | bytes 393224 | tf_op jit(solution)/shard_map/ppermute | solution.py:10
  64.2 8.4 %collective-permute-start.9 = (bf16[4,1,64,256]{3,2,1,0:T(8,128)(2,1)S(1)}, bf16[4,1,64,256]{3,2,1,0:T(8,128)(2,1)S(1)}, u32[]{:S(2)}, u32[]{:S(2)}) collective-permute-start(bf16[4,1,64,256]{3,2,1,0:T(8,128)(2,1)S(1)} %get-tuple-element.203), channel_id=1, source_target_pairs={{0,1},{1,2},{2,3},{3,4},{4,5},{5,6},{6,7},{7,8},{8,9},{9,10},{10,1... | collective-permute-start | bytes 393224 | tf_op jit(solution)/shard_map/ppermute | solution.py:21
  69.0 9.3 %collective-permute-start.10 = (bf16[4,1,64,256]{3,2,1,0:T(8,128)(2,1)S(1)}, bf16[4,1,64,256]{3,2,1,0:T(8,128)(2,1)S(1)}, u32[]{:S(2)}, u32[]{:S(2)}) collective-permute-start(bf16[4,1,64,256]{3,2,1,0:T(8,128)(2,1)S(1)} %get-tuple-element.204), channel_id=1, source_target_pairs={{1,0},{2,1},{3,2},{4,3},{5,4},{6,5},{7,6},{8,7},{9,8},{10,9},{11,1... | collective-permute-start | bytes 393224 | tf_op jit(solution)/shard_map/ppermute | solution.py:23
  78.4 16.8 %collective-permute-start.11 = (bf16[2,2,64,256]{3,2,1,0:T(8,128)(2,1)S(1)}, bf16[2,2,64,256]{3,2,1,0:T(8,128)(2,1)S(1)}, u32[]{:S(2)}, u32[]{:S(2)}) collective-permute-start(bf16[2,2,64,256]{3,2,1,0:T(8,128)(2,1)S(1)} %get-tuple-element.211), channel_id=1, source_target_pairs={{0,128},{128,256},{256,384},{1,129},{129,257},{257,385},{2,130},{1... | collective-permute-start | bytes 393224 | tf_op jit(solution)/shard_map/ppermute | solution.py:10
  95.5 7.7 %collective-permute-start.12 = (bf16[2,2,64,256]{3,2,1,0:T(8,128)(2,1)S(1)}, bf16[2,2,64,256]{3,2,1,0:T(8,128)(2,1)S(1)}, u32[]{:S(2)}, u32[]{:S(2)}) collective-permute-start(bf16[2,2,64,256]{3,2,1,0:T(8,128)(2,1)S(1)} %fusion.107), channel_id=1, source_target_pairs={{0,32},{32,64},{64,96},{1,33},{33,65},{65,97},{2,34},{34,66},{66,9... | collective-permute-start | bytes 393224 | tf_op jit(solution)/shard_map/ppermute | solution.py:10
  103.2 9.5 %collective-permute-start.13 = (bf16[4,1,64,256]{3,2,1,0:T(8,128)(2,1)S(1)}, bf16[4,1,64,256]{3,2,1,0:T(8,128)(2,1)S(1)}, u32[]{:S(2)}, u32[]{:S(2)}) collective-permute-start(bf16[4,1,64,256]{3,2,1,0:T(8,128)(2,1)S(1)} %get-tuple-element.201), channel_id=1, source_target_pairs={{0,1},{1,2},{2,3},{3,4},{4,5},{5,6},{6,7},{7,8},{8,9},{9,10},{10,1... | collective-permute-start | bytes 393224 | tf_op jit(solution)/shard_map/ppermute | solution.py:21
  107.2 9.3 %collective-permute-start.14 = (bf16[4,1,64,256]{3,2,1,0:T(8,128)(2,1)S(1)}, bf16[4,1,64,256]{3,2,1,0:T(8,128)(2,1)S(1)}, u32[]{:S(2)}, u32[]{:S(2)}) collective-permute-start(bf16[4,1,64,256]{3,2,1,0:T(8,128)(2,1)S(1)} %get-tuple-element.202), channel_id=1, source_target_pairs={{1,0},{2,1},{3,2},{4,3},{5,4},{6,5},{7,6},{8,7},{9,8},{10,9},{11,1... | collective-permute-start | bytes 393224 | tf_op jit(solution)/shard_map/ppermute | solution.py:23
  116.8 2.0 %copy-start.3 = (bf16[9,768,256]{2,1,0:T(8,128)(2,1)S(1)}, bf16[9,768,256]{2,1,0:T(8,128)(2,1)}, u32[]{:S(2)}) copy-start(bf16[9,768,256]{2,1,0:T(8,128)(2,1)} %get-tuple-element.58) | copy-start | bytes 10616836 | tf_op jit(solution)/shard_map/cond
where the time goes:
time: 123 us; the launch traced here: 122 us
  waiting for transfers between devices  72 us (59%)
  starting transfers between devices  40.9 us (33%)
  other arithmetic  4.22 us (3%)
  matrix products  2.42 us (2%)
  local copies, waits for them, and re-layouts  2.2 us (2%)
    ppermute x7, waiting for transfers between devices, passed_along(): return lax.ppermute(block, axis, route)  47.5 us
    ppermute x4, waiting for transfers between devices, padded_2(): lax.ppermute(head, axis, [((i + 1) % count, i) for i in range(ends)])  16.5 us
    ppermute x4, starting transfers between devices, padded_2(): lax.ppermute(tail, axis, [(i, (i + 1) % count) for i in range(ends)])  15.6 us
    ppermute x4, starting transfers between devices, padded_2(): lax.ppermute(head, axis, [((i + 1) % count, i) for i in range(ends)])  13.7 us
    ppermute x7, starting transfers between devices, passed_along(): return lax.ppermute(block, axis, route)  11.6 us
    ppermute x4, waiting for transfers between devices, padded_2(): lax.ppermute(tail, axis, [(i, (i + 1) % count) for i in range(ends)])  7.96 us
  transfers between devices with their start and end apart: 15, of which 15 were waited for; matrix products, arithmetic and copies ran while one was open for 0% of the time, Pallas kernels for 0%

commit v1 on v0

v1 whole, which is shorter than its diff:
```python
import functools

import jax
import jax.numpy as jnp
from jax import lax
from jax.experimental import pallas as pl
from jax.experimental.pallas import tpu as pltpu
from jax.sharding import PartitionSpec as P

MESH = pl.DeviceIdType.MESH
WORKER = 0
TAPS = 3


def chain_kernel(
    clip, weights, gains, out,
    x_in, hidden, filters, gain, rows_out,
    x_sem, home_sem, init_send, next_send, home_send, load_sem,
):
    section = lax.axis_index("section")
    tm = lax.axis_index("tm")
    space = lax.axis_index("space")
    sections = lax.axis_size("section")
    groups = lax.axis_size("tm")
    bands = lax.axis_size("space")
    run = tm // 2
    row = 2 * space + run
    last_row = 2 * bands - 1
    worker = tm % 2 == WORKER
    frames, _, columns, channels = clip.shape
    cells = frames * columns

    def row_device(at_section, at_row):
        at_section = jnp.clip(at_section, 0, sections - 1)
        at_row = jnp.clip(at_row, 0, last_row)
        return (at_section, 2 * (at_row % 2) + WORKER, at_row // 2)

    load_filters = pltpu.make_async_copy(weights.at[0], filters, load_sem.at[0])
    load_gain = pltpu.make_async_copy(gains, gain, load_sem.at[1])

    @pl.when(worker)
    def _():
        load_gain.start()
        load_filters.start()

    barrier = pltpu.get_barrier_semaphore()

    def greet(device):
        pl.semaphore_signal(barrier, inc=1, device_id=device, device_id_type=MESH)

    def init_targets():
        return (
            (None, 0, 2 * space, 1),
            (None, 1, 2 * space, 2),
            (None, 0, 2 * space + 1, 0),
            (None, 1, 2 * space + 1, 1),
            (space > 0, 0, 2 * space - 1, 2),
            (space < bands - 1, 1, 2 * space + 2, 0),
        )

    for group in range(groups):
        @pl.when((section == 0) & worker & (group != tm))
        def _(group=group):
            greet((0, group, space))

        @pl.when((section == 0) & worker & (run == 0) & (space > 0))
        def _(group=group):
            greet((0, group, jnp.maximum(space - 1, 0)))

        @pl.when((section == 0) & worker & (run == 1) & (space < bands - 1))
        def _(group=group):
            greet((0, group, jnp.minimum(space + 1, bands - 1)))

    for step in (-1, 0, 1):
        @pl.when((section > 0) & worker & (row + step >= 0) & (row + step <= last_row))
        def _(step=step):
            greet(row_device(section - 1, row + step))

    for near in range(2):
        @pl.when(tm != 2 * near + WORKER)
        def _(near=near):
            greet((section, 2 * near + WORKER, space))

    @pl.when(worker)
    def _():
        hidden[0:frames] = jnp.zeros((frames, *hidden.shape[1:]), hidden.dtype)

    @pl.when(worker & (row == 0))
    def _():
        x_in[:, 0] = jnp.zeros((groups, *x_in.shape[2:]), x_in.dtype)

    @pl.when(worker & (row == last_row))
    def _():
        x_in[:, 2] = jnp.zeros((groups, *x_in.shape[2:]), x_in.dtype)

    def has_next(step):
        return (section < sections - 1) & (row + step >= 0) & (row + step <= last_row)

    def one_if(condition):
        return jnp.where(condition, 1, 0)

    from_clip = one_if(section == 0) * (
        2 - one_if(worker) + one_if(space > 0) + one_if(space < bands - 1)
    )
    from_rows = one_if(worker) * (
        groups - 1 + one_if(has_next(-1)) + one_if(has_next(0)) + one_if(has_next(1))
    )
    receivers = from_clip + from_rows

    @pl.when(receivers > 0)
    def _():
        pl.semaphore_wait(barrier, receivers)

    def init_copies():
        copies = []
        for k, (condition, source, target, tap) in enumerate(init_targets()):
            own = (target % 2 == run) & worker & (k < 4)
            remote = pltpu.make_async_remote_copy(
                src_ref=clip.at[:, source],
                dst_ref=x_in.at[tm, tap],
                send_sem=init_send.at[k],
                recv_sem=x_sem.at[tm, tap],
                device_id=row_device(0, target),
                device_id_type=MESH,
            )
            local = pltpu.make_async_copy(clip.at[:, source], x_in.at[tm, tap], x_sem.at[tm, tap])
            copies.append((condition, own, remote, local))
        return copies

    @pl.when(section == 0)
    def _():
        for condition, own, remote, local in init_copies():
            if condition is None:
                @pl.when(own)
                def _(local=local):
                    local.start()

                @pl.when(jnp.logical_not(own))
                def _(remote=remote):
                    remote.start()
            else:
                @pl.when(condition)
                def _(remote=remote):
                    remote.start()

    def next_copy(group, step):
        return pltpu.make_async_remote_copy(
            src_ref=rows_out.at[group],
            dst_ref=x_in.at[group, 1 - step],
            send_sem=next_send.at[group, step + 1],
            recv_sem=x_sem.at[group, 1 - step],
            device_id=row_device(section + 1, row + step),
            device_id_type=MESH,
        )

    def home_copy(group):
        return pltpu.make_async_remote_copy(
            src_ref=rows_out.at[group],
            dst_ref=out.at[0, :, run],
            send_sem=home_send.at[group],
            recv_sem=home_sem.at[run],
            device_id=(section, group, space),
            device_id_type=MESH,
        )

    def own_copy(group):
        return pltpu.make_async_copy(rows_out.at[group], out.at[0, :, run], home_sem.at[run])

    def process(group, carry):
        first = group * frames
        for tap in (1, 0, 2):
            @pl.when((row + tap - 1 >= 0) & (row + tap - 1 <= last_row))
            def _(tap=tap):
                pltpu.make_async_copy(x_in.at[group, tap], x_in.at[group, tap], x_sem.at[group, tap]).wait()

            wide = x_in[group, tap].reshape(cells, channels).astype(jnp.float32)
            factor = lax.rsqrt(jnp.mean(wide * wide, axis=-1, keepdims=True) + 1e-06)
            value = wide * factor * gain[...]
            value = value / (1.0 + jnp.exp(-value))
            column = lax.broadcasted_iota(jnp.int32, value.shape, 0) % columns
            left = jnp.where(column == 0, 0.0, pltpu.roll(value, 1, 0))
            right = jnp.where(column == columns - 1, 0.0, pltpu.roll(value, cells - 1, 0))
            for part, shifted in enumerate((left, value, right)):
                hidden[pl.ds(first + frames, frames), tap, :, part * channels:(part + 1) * channels] = (
                    shifted.astype(jnp.bfloat16).reshape(frames, columns, channels)
                )

        @pl.when(group == 0)
        def _():
            load_filters.wait()

        total = x_in[group, 1].reshape(cells, channels).astype(jnp.float32)
        summed = jnp.zeros((cells, channels), jnp.float32)
        for time_tap in range(TAPS):
            for row_tap in range(TAPS):
                window = hidden[pl.ds(first + frames - 2 + time_tap, frames), row_tap]
                summed = summed + jnp.dot(
                    window.reshape(cells, TAPS * channels),
                    filters[TAPS * time_tap + row_tap],
                    preferred_element_type=jnp.float32,
                )
        rows_out[group] = (total + summed).astype(jnp.bfloat16).reshape(frames, columns, channels)

        for step in (-1, 1, 0):
            @pl.when(has_next(step))
            def _(step=step):
                next_copy(group, step).start()

        @pl.when(group == tm)
        def _():
            own_copy(group).start()

        @pl.when(group != tm)
        def _():
            home_copy(group).start()

        return carry

    @pl.when(worker)
    def _():
        load_gain.wait()
        lax.fori_loop(0, groups, process, 0)

    for near in range(2):
        arrived = out.at[0, :, near]
        pltpu.make_async_copy(arrived, arrived, home_sem.at[near]).wait()

    @pl.when(section == 0)
    def _():
        for condition, own, remote, _ in init_copies():
            needed = jnp.logical_not(own) if condition is None else condition

            @pl.when(needed)
            def _(remote=remote):
                remote.wait_send()

    def drain(group, carry):
        for step in (-1, 1, 0):
            @pl.when(has_next(step))
            def _(step=step):
                next_copy(group, step).wait_send()

        @pl.when(group != tm)
        def _():
            home_copy(group).wait_send()

        return carry

    @pl.when(worker)
    def _():
        lax.fori_loop(0, groups, drain, 0)


def on_device(clip_features, conv_kernels, norm_gains):
    frames, rows, columns, channels = clip_features.shape
    groups = lax.axis_size("tm")
    any_space = pl.BlockSpec(memory_space=pltpu.HBM)
    return pl.pallas_call(
        chain_kernel,
        out_shape=jax.ShapeDtypeStruct((1, frames, rows, columns, channels), jnp.bfloat16),
        in_specs=[any_space] * 3,
        out_specs=any_space,
        scratch_shapes=[
            pltpu.VMEM((groups, TAPS, frames, columns, channels), jnp.bfloat16),
            pltpu.VMEM(((groups + 1) * frames, TAPS, columns, TAPS * channels), jnp.bfloat16),
            pltpu.VMEM(conv_kernels.shape[1:], jnp.bfloat16),
            pltpu.VMEM(norm_gains.shape, jnp.float32),
            pltpu.VMEM((groups, frames, columns, channels), jnp.bfloat16),
            pltpu.SemaphoreType.DMA((groups, TAPS)),
            pltpu.SemaphoreType.DMA((2,)),
            pltpu.SemaphoreType.DMA((6,)),
            pltpu.SemaphoreType.DMA((groups, TAPS)),
            pltpu.SemaphoreType.DMA((groups,)),
            pltpu.SemaphoreType.DMA((2,)),
        ],
        compiler_params=pltpu.CompilerParams(
            collective_id=0, has_side_effects=True, vmem_limit_bytes=56 * 2**20
        ),
        name="chain",
    )(clip_features, conv_kernels, norm_gains)


def solution(mesh):
    return jax.shard_map(
        on_device,
        mesh=mesh,
        in_specs=(P("tm", "space", None, None), P("section", None, None, None), P("section", None)),
        out_specs=P("section", "tm", "space", None, None),
        check_vma=False,
    )
```

time: 123 us -> 46.9 us (0.38)
  the two profiles are of different devices: /device:TPU:222 before, /device:TPU:383 now
where the time goes in v1:
time: 46.9 us; the launch traced here: 46.8 us
  Pallas kernels  45.2 us (96%)
  local copies, waits for them, and re-layouts  1.57 us (3%)
    pallas_call x1, Pallas kernels, on_device(): pl.pallas_call(chain_kernel, out_shape=jax.ShapeDtypeStruct((1, frames, r...  45.2 us
    unnamed x1, local copies, waits for them, and re-layouts  1.57 us

profile of v1, /device:TPU:383, one launch (start us, length us, event | category | flops | bytes accessed | tf_op | source)
XLA Modules:
  0.0 46.8 jit_solution(12360605157973718004)
XLA Ops:
  0.0 45.2 %chain.1 = bf16[1,2,2,64,256]{4,3,2,1,0:T(8,128)(2,1)} custom-call(bf16[2,2,64,256]{3,2,1,0:T(8,128)(2,1)} %clip.1, bf16[1,9,768,256]{3,2,1,0:T(8,128)(2,1)} %weights.1, f32[1,256]{1,0:T(1,128)} %gains.1), custom_call_target="tpu_custom_call" | custom-call | tf_op jit(solution)/shard_map/chain/pallas_call | solution.py:258
  45.2 1.6 %copy.5 = bf16[1,2,2,64,256]{4,3,2,1,0:T(8,128)(2,1)} copy(bf16[1,2,2,64,256]{4,3,2,1,0:T(8,128)(2,1)} %chain.1) | data formatting | bytes 262144

commit v2 on v1

--- a/solution.py
+++ b/solution.py
@@ -8,7 +8,7 @@
 from jax.sharding import PartitionSpec as P
 
 MESH = pl.DeviceIdType.MESH
-WORKER = 0
+WORKER = 1
 TAPS = 3
 
 
@@ -58,18 +58,21 @@
             (space < bands - 1, 1, 2 * space + 2, 0),
         )
 
+    sender = section == tm % sections
     for group in range(groups):
-        @pl.when((section == 0) & worker & (group != tm))
-        def _(group=group):
-            greet((0, group, space))
+        source = group % sections
+
+        @pl.when((section == 0) & worker & ((source != 0) | (group != tm)))
+        def _(group=group, source=source):
+            greet((source, group, space))
 
         @pl.when((section == 0) & worker & (run == 0) & (space > 0))
-        def _(group=group):
-            greet((0, group, jnp.maximum(space - 1, 0)))
+        def _(group=group, source=source):
+            greet((source, group, jnp.maximum(space - 1, 0)))
 
         @pl.when((section == 0) & worker & (run == 1) & (space < bands - 1))
-        def _(group=group):
-            greet((0, group, jnp.minimum(space + 1, bands - 1)))
+        def _(group=group, source=source):
+            greet((source, group, jnp.minimum(space + 1, bands - 1)))
 
     for step in (-1, 0, 1):
         @pl.when((section > 0) & worker & (row + step >= 0) & (row + step <= last_row))
@@ -99,8 +102,8 @@
     def one_if(condition):
         return jnp.where(condition, 1, 0)
 
-    from_clip = one_if(section == 0) * (
-        2 - one_if(worker) + one_if(space > 0) + one_if(space < bands - 1)
+    from_clip = one_if(sender) * (
+        2 - one_if(worker & (section == 0)) + one_if(space > 0) + one_if(space < bands - 1)
     )
     from_rows = one_if(worker) * (
         groups - 1 + one_if(has_next(-1)) + one_if(has_next(0)) + one_if(has_next(1))
@@ -114,7 +117,7 @@
     def init_copies():
         copies = []
         for k, (condition, source, target, tap) in enumerate(init_targets()):
-            own = (target % 2 == run) & worker & (k < 4)
+            own = (section == 0) & (target % 2 == run) & worker & (k < 4)
             remote = pltpu.make_async_remote_copy(
                 src_ref=clip.at[:, source],
                 dst_ref=x_in.at[tm, tap],
@@ -127,7 +130,7 @@
             copies.append((condition, own, remote, local))
         return copies
 
-    @pl.when(section == 0)
+    @pl.when(sender)
     def _():
         for condition, own, remote, local in init_copies():
             if condition is None:
@@ -225,7 +228,7 @@
         arrived = out.at[0, :, near]
         pltpu.make_async_copy(arrived, arrived, home_sem.at[near]).wait()
 
-    @pl.when(section == 0)
+    @pl.when(sender)
     def _():
         for condition, own, remote, _ in init_copies():
             needed = jnp.logical_not(own) if condition is None else condition

time: 46.9 us -> 39.4 us (0.84)
  the two profiles are of different devices: /device:TPU:383 before, /device:TPU:31 now
where the time goes in v2:
time: 39.4 us; the launch traced here: 39.2 us
  Pallas kernels  37.7 us (96%)
  local copies, waits for them, and re-layouts  1.57 us (4%)
    pallas_call x1, Pallas kernels, on_device(): pl.pallas_call(chain_kernel, out_shape=jax.ShapeDtypeStruct((1, frames, r...  37.7 us
    unnamed x1, local copies, waits for them, and re-layouts  1.57 us

profile of v2, /device:TPU:31, one launch (start us, length us, event | category | flops | bytes accessed | tf_op | source)
XLA Modules:
  0.0 39.2 jit_solution(7905516104755545437)
XLA Ops:
  0.0 37.7 %chain.1 = bf16[1,2,2,64,256]{4,3,2,1,0:T(8,128)(2,1)} custom-call(bf16[2,2,64,256]{3,2,1,0:T(8,128)(2,1)} %clip.1, bf16[1,9,768,256]{3,2,1,0:T(8,128)(2,1)} %weights.1, f32[1,256]{1,0:T(1,128)} %gains.1), custom_call_target="tpu_custom_call" | custom-call | tf_op jit(solution)/shard_map/chain/pallas_call | solution.py:261
  37.7 1.6 %copy.5 = bf16[1,2,2,64,256]{4,3,2,1,0:T(8,128)(2,1)} copy(bf16[1,2,2,64,256]{4,3,2,1,0:T(8,128)(2,1)} %chain.1) | data formatting | bytes 262144

commit v3 on v0

v3 whole, which is shorter than its diff:
```python
import jax
import jax.numpy as jnp
from jax import lax
from jax.experimental import pallas as pl
from jax.experimental.pallas import tpu as pltpu
from jax.sharding import PartitionSpec as P

MESH = pl.DeviceIdType.MESH
WORKER = 1
TAPS = 3
TALL = 4
TILES = 4
LANES = 128


def chain_kernel(
    clip, weights, gains, out,
    own_in, row_in, edge_in, hidden, halo, filters, gain, wide_out, tile_out, edge_out,
    clip_in, clip_wide, clip_edge,
    own_sem, row_sem, edge_sem, home_sem, clip_send, next_send, home_send, load_sem,
):
    section = lax.axis_index("section")
    tm = lax.axis_index("tm")
    space = lax.axis_index("space")
    sections = lax.axis_size("section")
    groups = lax.axis_size("tm")
    bands = lax.axis_size("space") // 2
    band = space // 2
    half = space % 2
    tile = 2 * half + tm // 2
    worker = tm % 2 == WORKER
    sender = section == tm % sections
    frames, pair, columns, channels = clip.shape
    wide = columns // TILES
    cells = frames * TALL * wide
    edge_cells = frames * TALL
    beside = band + 2 * half - 1
    has_beside = (beside >= 0) & (beside < bands)

    def worker_device(at_section, at_tile, at_band):
        at_section = jnp.clip(at_section, 0, sections - 1)
        at_tile = jnp.clip(at_tile, 0, TILES - 1)
        at_band = jnp.clip(at_band, 0, bands - 1)
        return (at_section, 2 * (at_tile % 2) + WORKER, 2 * at_band + at_tile // 2)

    def inside(step_tile, step_band):
        there = None
        for at, step, end in ((tile, step_tile, TILES), (band, step_band, bands)):
            if step:
                here = (at > 0) if step < 0 else (at < end - 1)
                there = here if there is None else there & here
        return there

    def when(condition, action):
        if condition is None:
            action()
        else:
            pl.when(condition)(action)

    barrier = pltpu.get_barrier_semaphore()

    def greet(device):
        pl.semaphore_signal(barrier, inc=1, device_id=device, device_id_type=MESH)

    @pl.when(worker & (section == 0))
    def _():
        for group in range(groups):
            for near in range(2):
                greet((group % sections, group, 2 * band + near))

        @pl.when(band > 0)
        def _():
            for group in range(groups):
                greet((group % sections, group, jnp.maximum(2 * band - 1, 0)))

        @pl.when(band < bands - 1)
        def _():
            for group in range(groups):
                greet((group % sections, group, jnp.minimum(2 * band + 2, 2 * bands - 1)))

    load_filters = pltpu.make_async_copy(weights.at[0], filters, load_sem.at[0])
    load_gain = pltpu.make_async_copy(gains, gain, load_sem.at[1])
    load_clip = pltpu.make_async_copy(clip, clip_in, load_sem.at[2])

    @pl.when(sender)
    def _():
        load_clip.start()

    @pl.when(worker)
    def _():
        load_gain.start()
        load_filters.start()

    steps = [(t, b) for t in (-1, 1, 0) for b in (-1, 1, 0)]

    @pl.when(worker & (section > 0))
    def _():
        for t, b in steps:
            when(inside(t, b), lambda t=t, b=b: greet(worker_device(section - 1, tile + t, band + b)))

    for near in range(TILES):
        @pl.when(jnp.logical_not(worker & (tile == near)))
        def _(near=near):
            greet(worker_device(section, near, band))

    @pl.when(worker)
    def _():
        hidden[0:frames] = jnp.zeros((frames, *hidden.shape[1:]), hidden.dtype)

        @pl.when(band == 0)
        def _():
            row_in[:, 0] = jnp.zeros((groups, *row_in.shape[2:]), row_in.dtype)
            edge_in[:, :, 0] = jnp.zeros((groups, 2, *edge_in.shape[3:]), edge_in.dtype)

        @pl.when(band == bands - 1)
        def _():
            row_in[:, 1] = jnp.zeros((groups, *row_in.shape[2:]), row_in.dtype)
            edge_in[:, :, 3] = jnp.zeros((groups, 2, *edge_in.shape[3:]), edge_in.dtype)

        @pl.when(section > 0)
        def _():
            edge_in[:, :, 2] = jnp.zeros((groups, 2, *edge_in.shape[3:]), edge_in.dtype)

        @pl.when(tile == 0)
        def _():
            edge_in[:, 0] = jnp.zeros((groups, *edge_in.shape[2:]), edge_in.dtype)

        @pl.when(tile == TILES - 1)
        def _():
            edge_in[:, 1] = jnp.zeros((groups, *edge_in.shape[2:]), edge_in.dtype)

    left_edges = [(0, at, at * wide - 1) for at in range(1, TILES)]
    right_edges = [(1, at, at * wide + wide) for at in range(TILES - 1)]
    clip_edges = left_edges + right_edges

    @pl.when(sender)
    def _():
        load_clip.wait()
        for n in range(channels // LANES):
            clip_wide[n] = clip_in[:, :, :, n * LANES:(n + 1) * LANES].reshape(-1, LANES).astype(jnp.float32)
        for n, (_, _, column) in enumerate(clip_edges):
            parts = []
            for lane in range(channels // LANES):
                part = clip_wide[lane, pl.ds(column, frames * pair, stride=columns), :]
                parts += [part, part]
            clip_edge[n] = jnp.concatenate(parts, axis=0).astype(jnp.bfloat16)

    def one_if(condition):
        return jnp.where(condition, 1, 0)

    near_tiles = 1 + one_if(tile > 0) + one_if(tile < TILES - 1)
    near_bands = 1 + one_if(band > 0) + one_if(band < bands - 1)
    receivers = (
        one_if(sender) * TILES * (1 + one_if(has_beside))
        + one_if(worker) * (2 * groups - 1 + one_if(section < sections - 1) * near_tiles * near_bands)
    )

    @pl.when(receivers > 0)
    def _():
        pl.semaphore_wait(barrier, receivers)

    def clip_copies():
        copies = []

        def add(condition, source, target, arrived, at_tile, at_band):
            copies.append((condition, pltpu.make_async_remote_copy(
                src_ref=source,
                dst_ref=target,
                send_sem=clip_send.at[len(copies)],
                recv_sem=arrived,
                device_id=worker_device(0, at_tile, at_band),
                device_id_type=MESH,
            )))

        for n, (side, at, _) in enumerate(clip_edges):
            piece = 3 * (1 - half)
            add(has_beside, clip_edge.at[n], edge_in.at[tm, side, piece], edge_sem.at[tm, side, piece], at, beside)
        for at in range(TILES):
            add(has_beside, clip.at[:, half, at * wide:(at + 1) * wide], row_in.at[tm, 1 - half],
                row_sem.at[tm, 1 - half], at, beside)
        for n, (side, at, _) in enumerate(clip_edges):
            piece = 1 + half
            add(None, clip_edge.at[n], edge_in.at[tm, side, piece], edge_sem.at[tm, side, piece], at, band)
        for at in range(TILES):
            add(None, clip.at[:, :, at * wide:(at + 1) * wide], own_in.at[tm, :, pl.ds(pair * half, pair)],
                own_sem.at[tm, half], at, band)
        return copies

    @pl.when(sender)
    def _():
        for condition, copy in clip_copies():
            when(condition, copy.start)

    def next_copies(group):
        copies = []
        for n, (t, b) in enumerate(steps):
            if t:
                side, piece = (1 if t < 0 else 0), {-1: 3, 0: 1, 1: 0}[b]
                source = edge_out.at[group, 1 - side]
                target, arrived = edge_in.at[group, side, piece], edge_sem.at[group, side, piece]
            elif b:
                source = tile_out.at[group, :, 0 if b < 0 else TALL - 1]
                above = 1 if b < 0 else 0
                target, arrived = row_in.at[group, above], row_sem.at[group, above]
            else:
                source, target, arrived = tile_out.at[group], own_in.at[group], own_sem.at[group, 0]
            copies.append((inside(t, b), pltpu.make_async_remote_copy(
                src_ref=source,
                dst_ref=target,
                send_sem=next_send.at[group, n],
                recv_sem=arrived,
                device_id=worker_device(section + 1, tile + t, band + b),
                device_id_type=MESH,
            )))
        return copies

    def home_target():
        return out.at[0, :, :, pl.ds(pl.multiple_of(tile * wide, wide), wide)]

    def home_copy(group, near):
        return pltpu.make_async_remote_copy(
            src_ref=tile_out.at[group, :, near * pair:(near + 1) * pair],
            dst_ref=home_target(),
            send_sem=home_send.at[group, near],
            recv_sem=home_sem.at[tile],
            device_id=(section, group, 2 * band + near),
            device_id_type=MESH,
        )

    def own_copy(group, near):
        source = tile_out.at[group, :, near * pair:(near + 1) * pair]
        return pltpu.make_async_copy(source, home_target(), home_sem.at[tile])

    def arrived(ref, sem):
        pltpu.make_async_copy(ref, ref, sem).wait()

    def activated(value):
        factor = lax.rsqrt(jnp.mean(value * value, axis=-1, keepdims=True) + 1e-06)
        value = value * factor * gain[...]
        return value / (1.0 + jnp.exp(-value))

    def process(group, carry):
        first = group * frames

        for side, t in ((0, -1), (1, 1)):
            for piece, b in ((0, -1), (1, 0), (3, 1)):
                when(inside(t, b), lambda side=side, piece=piece: arrived(
                    edge_in.at[group, side, piece], edge_sem.at[group, side, piece]))

            @pl.when((section == 0) & inside(t, 0))
            def _(side=side):
                arrived(edge_in.at[group, side, 2], edge_sem.at[group, side, 2])

        for above, b in ((0, -1), (1, 1)):
            when(inside(0, b), lambda above=above: arrived(row_in.at[group, above], row_sem.at[group, above]))

        @pl.when(section == 0)
        def _():
            for near in range(2):
                arrived(own_in.at[group, :, near * pair:(near + 1) * pair], own_sem.at[group, near])

        @pl.when(section > 0)
        def _():
            arrived(own_in.at[group], own_sem.at[group, 0])

        lower = lax.broadcasted_iota(jnp.int32, (edge_cells, channels), 0) >= edge_cells // 2
        pieces = []
        for side in range(2):
            above, middle, under, below = (
                jnp.concatenate(
                    [edge_in[group, side, p][n * edge_cells:(n + 1) * edge_cells].astype(jnp.float32)
                     for n in range(channels // LANES)],
                    axis=1,
                )
                for p in range(4)
            )
            pieces += [above, jnp.where(lower & (section == 0), under, middle), below]
        halo[...] = activated(jnp.concatenate(pieces, axis=0))

        own = own_in[group].reshape(cells, channels).astype(jnp.float32)
        middle = activated(own).reshape(frames, TALL, wide, channels)
        outer = activated(row_in[group].reshape(2 * frames * wide, channels).astype(jnp.float32))
        outer = outer.reshape(2, frames, wide, channels)
        column = lax.broadcasted_iota(jnp.int32, (wide, channels), 0)
        for frame in range(frames):
            for row in range(TALL + 2):
                if row == 0:
                    here, at = outer[0, frame], edge_cells // 2 + pair * frame + pair - 1
                elif row == TALL + 1:
                    here, at = outer[1, frame], 2 * edge_cells + pair * frame
                else:
                    part, within = divmod(row - 1, pair)
                    here = middle[frame, row - 1]
                    at = edge_cells + part * (edge_cells // 2) + pair * frame + within
                left = jnp.where(column == 0, halo[pl.ds(at, 1), :], pltpu.roll(here, 1, 0))
                at += TAPS * edge_cells
                right = jnp.where(column == wide - 1, halo[pl.ds(at, 1), :], pltpu.roll(here, wide - 1, 0))
                for part, shifted in enumerate((left, here, right)):
                    hidden[first + frames + frame, row, :, part * channels:(part + 1) * channels] = (
                        shifted.astype(jnp.bfloat16)
                    )

        @pl.when(group == 0)
        def _():
            load_filters.wait()

        summed = jnp.zeros((cells, channels), jnp.float32)
        for time_tap in range(TAPS):
            for row_tap in range(TAPS):
                window = hidden[pl.ds(first + frames - 2 + time_tap, frames), row_tap:row_tap + TALL]
                summed = summed + jnp.dot(
                    window.reshape(cells, TAPS * channels),
                    filters[TAPS * time_tap + row_tap],
                    preferred_element_type=jnp.float32,
                )
        result = own + summed
        tile_out[group] = result.astype(jnp.bfloat16).reshape(frames, TALL, wide, channels)

        @pl.when(section < sections - 1)
        def _():
            block = pair * wide
            for frame in range(frames):
                for part in range(TALL // pair):
                    source = (frame * (TALL // pair) + part) * block
                    for n in range(channels // LANES):
                        wide_out[n, pl.ds((part * frames + frame) * block, block), :] = (
                            result[source:source + block, n * LANES:(n + 1) * LANES]
                        )
            for side, at in enumerate((0, wide - 1)):
                parts = [
                    wide_out[n, pl.ds(at, edge_cells, stride=wide), :]
                    for n in range(channels // LANES)
                ]
                edge_out[group, side] = jnp.concatenate(parts, axis=0).astype(jnp.bfloat16)
            for condition, copy in next_copies(group):
                when(condition, copy.start)

        for near in range(2):
            own_home = (group == tm) & (near == half)

            @pl.when(own_home)
            def _(near=near):
                own_copy(group, near).start()

            @pl.when(jnp.logical_not(own_home))
            def _(near=near):
                home_copy(group, near).start()

        return carry

    @pl.when(worker)
    def _():
        load_gain.wait()
        lax.fori_loop(0, groups, process, 0)

    for at in range(TILES):
        arrived(out.at[0, :, :, at * wide:(at + 1) * wide], home_sem.at[at])

    @pl.when(sender)
    def _():
        for condition, copy in clip_copies():
            when(condition, copy.wait_send)

    def drain(group, carry):
        @pl.when(section < sections - 1)
        def _():
            for condition, copy in next_copies(group):
                when(condition, copy.wait_send)

        for near in range(2):
            @pl.when(jnp.logical_not((group == tm) & (near == half)))
            def _(near=near):
                home_copy(group, near).wait_send()

        return carry

    @pl.when(worker)
    def _():
        lax.fori_loop(0, groups, drain, 0)


def on_device(clip_features, conv_kernels, norm_gains):
    frames, pair, columns, channels = clip_features.shape
    groups = lax.axis_size("tm")
    wide = columns // TILES
    edge_cells = frames * TALL
    edge = (edge_cells * channels // LANES, LANES)
    edges = 2 * (TILES - 1)
    in_hbm = pl.BlockSpec(memory_space=pltpu.HBM)
    return pl.pallas_call(
        chain_kernel,
        out_shape=jax.ShapeDtypeStruct((1, frames, pair, columns, channels), jnp.bfloat16),
        in_specs=[in_hbm] * 3,
        out_specs=in_hbm,
        scratch_shapes=[
            pltpu.VMEM((groups, frames, TALL, wide, channels), jnp.bfloat16),
            pltpu.VMEM((groups, 2, frames, wide, channels), jnp.bfloat16),
            pltpu.VMEM((groups, 2, 4, *edge), jnp.bfloat16),
            pltpu.VMEM(((groups + 1) * frames, TALL + 2, wide, TAPS * channels), jnp.bfloat16),
            pltpu.VMEM((2 * TAPS * edge_cells, channels), jnp.float32),
            pltpu.VMEM(conv_kernels.shape[1:], jnp.bfloat16),
            pltpu.VMEM(norm_gains.shape, jnp.float32),
            pltpu.VMEM((channels // LANES, frames * TALL * wide, LANES), jnp.float32),
            pltpu.VMEM((groups, frames, TALL, wide, channels), jnp.bfloat16),
            pltpu.VMEM((groups, 2, *edge), jnp.bfloat16),
            pltpu.VMEM((frames, pair, columns, channels), jnp.bfloat16),
            pltpu.VMEM((channels // LANES, frames * pair * columns, LANES), jnp.float32),
            pltpu.VMEM((edges, *edge), jnp.bfloat16),
            pltpu.SemaphoreType.DMA((groups, 2)),
            pltpu.SemaphoreType.DMA((groups, 2)),
            pltpu.SemaphoreType.DMA((groups, 2, 4)),
            pltpu.SemaphoreType.DMA((TILES,)),
            pltpu.SemaphoreType.DMA((2 * edges + 2 * TILES,)),
            pltpu.SemaphoreType.DMA((groups, 9)),
            pltpu.SemaphoreType.DMA((groups, 2)),
            pltpu.SemaphoreType.DMA((3,)),
        ],
        compiler_params=pltpu.CompilerParams(
            collective_id=0, has_side_effects=True, vmem_limit_bytes=56 * 2**20
        ),
        name="chain",
    )(clip_features, conv_kernels, norm_gains)


def solution(mesh):
    return jax.shard_map(
        on_device,
        mesh=mesh,
        in_specs=(P("tm", "space", None, None), P("section", None, None, None), P("section", None)),
        out_specs=P("section", "tm", "space", None, None),
        check_vma=False,
    )
```

time: 123 us -> 32.4 us (0.26)
  the two profiles are of different devices: /device:TPU:222 before, /device:TPU:123 now
where the time goes in v3:
time: 32.4 us; the launch traced here: 32.3 us
  Pallas kernels  30.7 us (95%)
  local copies, waits for them, and re-layouts  1.57 us (5%)
    pallas_call x1, Pallas kernels, on_device(): pl.pallas_call(chain_kernel, out_shape=jax.ShapeDtypeStruct((1, frames, p...  30.7 us
    unnamed x1, local copies, waits for them, and re-layouts  1.57 us

profile of v3, /device:TPU:123, one launch (start us, length us, event | category | flops | bytes accessed | tf_op | source)
XLA Modules:
  0.0 32.3 jit_solution(11973380011472192086)
XLA Ops:
  0.0 30.7 %chain.1 = bf16[1,2,2,64,256]{4,3,2,1,0:T(8,128)(2,1)} custom-call(bf16[2,2,64,256]{3,2,1,0:T(8,128)(2,1)} %clip.1, bf16[1,9,768,256]{3,2,1,0:T(8,128)(2,1)} %weights.1, f32[1,256]{1,0:T(1,128)} %gains.1), custom_call_target="tpu_custom_call" | custom-call | tf_op jit(solution)/shard_map/chain/pallas_call | solution.py:390
  30.7 1.6 %copy.5 = bf16[1,2,2,64,256]{4,3,2,1,0:T(8,128)(2,1)} copy(bf16[1,2,2,64,256]{4,3,2,1,0:T(8,128)(2,1)} %chain.1) | data formatting | bytes 262144

commit v4 on v3

--- a/solution.py
+++ b/solution.py
@@ -387,7 +387,7 @@
     edge = (edge_cells * channels // LANES, LANES)
     edges = 2 * (TILES - 1)
     in_hbm = pl.BlockSpec(memory_space=pltpu.HBM)
-    return pl.pallas_call(
+    blocks = pl.pallas_call(
         chain_kernel,
         out_shape=jax.ShapeDtypeStruct((1, frames, pair, columns, channels), jnp.bfloat16),
         in_specs=[in_hbm] * 3,
@@ -420,6 +420,7 @@
         ),
         name="chain",
     )(clip_features, conv_kernels, norm_gains)
+    return jnp.clip(blocks, jnp.finfo(jnp.bfloat16).min, jnp.finfo(jnp.bfloat16).max)
 
 
 def solution(mesh):

time: 32.4 us -> 32.4 us (level)
  other arithmetic: 0 us -> 1.57 us
  local copies, waits for them, and re-layouts: 1.57 us -> 0 us
    min x0 -> x1, other arithmetic: none -> 1.57 us  [on_device(): jnp.clip(blocks, jnp.finfo(jnp.bfloat16).min, jnp.finfo(jnp.bfloat16).max)]
    unnamed x1 -> x0, local copies, waits for them, and re-layouts: 1.57 us -> none
where the time goes in v4:
time: 32.4 us; the launch traced here: 32.3 us
  Pallas kernels  30.7 us (95%)
  other arithmetic  1.57 us (5%)
    pallas_call x1, Pallas kernels, on_device(): pl.pallas_call(chain_kernel, out_shape=jax.ShapeDtypeStruct((1, frames, p...  30.7 us
    min x1, other arithmetic, on_device(): jnp.clip(blocks, jnp.finfo(jnp.bfloat16).min, jnp.finfo(jnp.bfloat16).max)  1.57 us

profile of v4, /device:TPU:123, one launch (start us, length us, event | category | flops | bytes accessed | tf_op | source)
XLA Modules:
  0.0 32.3 jit_solution(7558837698206991822)
XLA Ops:
  0.0 30.7 %chain.1 = bf16[1,2,2,64,256]{4,3,2,1,0:T(8,128)(2,1)} custom-call(bf16[2,2,64,256]{3,2,1,0:T(8,128)(2,1)} %clip.1, bf16[1,9,768,256]{3,2,1,0:T(8,128)(2,1)} %weights.1, f32[1,256]{1,0:T(1,128)} %gains.1), custom_call_target="tpu_custom_call" | custom-call | tf_op jit(solution)/shard_map/chain/pallas_call | solution.py:390
  30.7 1.6 %broadcast_clamp_fusion = bf16[1,2,2,64,256]{4,3,2,1,0:T(8,128)(2,1)} fusion(bf16[1,2,2,64,256]{4,3,2,1,0:T(8,128)(2,1)} %chain.1), kind=kLoop, calls=%fused_computation | loop fusion | flops 65536 | bytes 262144 | tf_op jit(solution)/shard_map/jit(clip)/min | solution.py:423

commit v5 on v3

v5 whole, which is shorter than its diff:
```python
import jax
import jax.numpy as jnp
from jax import lax
from jax.experimental import pallas as pl
from jax.experimental.pallas import tpu as pltpu
from jax.sharding import PartitionSpec as P

MESH = pl.DeviceIdType.MESH
WORKER = 1
TAPS = 3
TALL = 4
TILES = 4
LANES = 128


def chain_kernel(
    clip, weights, gains, out,
    own_in, row_in, edge_in, hidden, partial, halo, filters, gain, wide_out, tile_out, edge_out,
    clip_in, clip_wide, clip_edge,
    own_sem, row_sem, edge_sem, home_sem, clip_send, next_send, home_send, load_sem,
):
    section = lax.axis_index("section")
    tm = lax.axis_index("tm")
    space = lax.axis_index("space")
    sections = lax.axis_size("section")
    groups = lax.axis_size("tm")
    bands = lax.axis_size("space") // 2
    band = space // 2
    half = space % 2
    tile = 2 * half + tm // 2
    worker = tm % 2 == WORKER
    sender = section == tm % sections
    frames, pair, columns, channels = clip.shape
    wide = columns // TILES
    cells = TALL * wide
    ahead = TAPS - 1
    last_group = groups - 1
    total_units = last_group + frames
    edge_cells = frames * TALL
    beside = band + 2 * half - 1
    has_beside = (beside >= 0) & (beside < bands)

    def worker_device(at_section, at_tile, at_band):
        at_section = jnp.clip(at_section, 0, sections - 1)
        at_tile = jnp.clip(at_tile, 0, TILES - 1)
        at_band = jnp.clip(at_band, 0, bands - 1)
        return (at_section, 2 * (at_tile % 2) + WORKER, 2 * at_band + at_tile // 2)

    def inside(step_tile, step_band):
        there = None
        for at, step, end in ((tile, step_tile, TILES), (band, step_band, bands)):
            if step:
                here = (at > 0) if step < 0 else (at < end - 1)
                there = here if there is None else there & here
        return there

    def when(condition, action):
        if condition is None:
            action()
        else:
            pl.when(condition)(action)

    barrier = pltpu.get_barrier_semaphore()

    def greet(device):
        pl.semaphore_signal(barrier, inc=1, device_id=device, device_id_type=MESH)

    @pl.when(worker & (section == 0))
    def _():
        for group in range(groups):
            for near in range(2):
                greet((group % sections, group, 2 * band + near))

        @pl.when(band > 0)
        def _():
            for group in range(groups):
                greet((group % sections, group, jnp.maximum(2 * band - 1, 0)))

        @pl.when(band < bands - 1)
        def _():
            for group in range(groups):
                greet((group % sections, group, jnp.minimum(2 * band + 2, 2 * bands - 1)))

    load_filters = pltpu.make_async_copy(weights.at[0], filters, load_sem.at[0])
    load_gain = pltpu.make_async_copy(gains, gain, load_sem.at[1])
    load_clip = pltpu.make_async_copy(clip, clip_in, load_sem.at[2])

    @pl.when(sender)
    def _():
        load_clip.start()

    @pl.when(worker)
    def _():
        load_gain.start()
        load_filters.start()

    steps = [(t, b) for t in (-1, 1, 0) for b in (-1, 1, 0)]

    @pl.when(worker & (section > 0))
    def _():
        for t, b in steps:
            when(inside(t, b), lambda t=t, b=b: greet(worker_device(section - 1, tile + t, band + b)))

    for near in range(TILES):
        @pl.when(jnp.logical_not(worker & (tile == near)))
        def _(near=near):
            greet(worker_device(section, near, band))

    @pl.when(worker)
    def _():
        hidden[0:ahead] = jnp.zeros((ahead, *hidden.shape[1:]), hidden.dtype)
        partial[...] = jnp.zeros_like(partial)

        @pl.when(band == 0)
        def _():
            row_in[0] = jnp.zeros(row_in.shape[1:], row_in.dtype)
            edge_in[:, :, 0] = jnp.zeros((total_units, 2, *edge_in.shape[3:]), edge_in.dtype)

        @pl.when(band == bands - 1)
        def _():
            row_in[1] = jnp.zeros(row_in.shape[1:], row_in.dtype)
            edge_in[:, :, 3] = jnp.zeros((total_units, 2, *edge_in.shape[3:]), edge_in.dtype)

        @pl.when(section > 0)
        def _():
            edge_in[:, :, 2] = jnp.zeros((total_units, 2, *edge_in.shape[3:]), edge_in.dtype)

        @pl.when(tile == 0)
        def _():
            edge_in[:, 0] = jnp.zeros((total_units, *edge_in.shape[2:]), edge_in.dtype)

        @pl.when(tile == TILES - 1)
        def _():
            edge_in[:, 1] = jnp.zeros((total_units, *edge_in.shape[2:]), edge_in.dtype)

    left_edges = [(0, at, at * wide - 1) for at in range(1, TILES)]
    right_edges = [(1, at, at * wide + wide) for at in range(TILES - 1)]
    clip_edges = left_edges + right_edges

    @pl.when(sender)
    def _():
        load_clip.wait()
        for n in range(channels // LANES):
            clip_wide[n] = clip_in[:, :, :, n * LANES:(n + 1) * LANES].reshape(-1, LANES).astype(jnp.float32)
        for n, (_, _, column) in enumerate(clip_edges):
            parts = []
            for lane in range(channels // LANES):
                part = clip_wide[lane, pl.ds(column, frames * pair, stride=columns), :]
                parts += [part, part]
            clip_edge[n] = jnp.concatenate(parts, axis=0).astype(jnp.bfloat16)

    def one_if(condition):
        return jnp.where(condition, 1, 0)

    near_tiles = 1 + one_if(tile > 0) + one_if(tile < TILES - 1)
    near_bands = 1 + one_if(band > 0) + one_if(band < bands - 1)
    receivers = (
        one_if(sender) * TILES * (1 + one_if(has_beside))
        + one_if(worker) * (2 * groups - 1 + one_if(section < sections - 1) * near_tiles * near_bands)
    )

    @pl.when(receivers > 0)
    def _():
        pl.semaphore_wait(barrier, receivers)

    def clip_copies():
        copies = []

        def add(condition, source, target, arrived, at_tile, at_band):
            copies.append((condition, pltpu.make_async_remote_copy(
                src_ref=source,
                dst_ref=target,
                send_sem=clip_send.at[len(copies)],
                recv_sem=arrived,
                device_id=worker_device(0, at_tile, at_band),
                device_id_type=MESH,
            )))

        for n, (side, at, _) in enumerate(clip_edges):
            piece = 3 * (1 - half)
            add(has_beside, clip_edge.at[n], edge_in.at[tm, side, piece], edge_sem.at[tm, side, piece], at, beside)
        for at in range(TILES):
            add(has_beside, clip_in.at[:, half, at * wide:(at + 1) * wide],
                row_in.at[1 - half, pl.ds(tm * frames, frames)],
                row_sem.at[tm, 1 - half], at, beside)
        for n, (side, at, _) in enumerate(clip_edges):
            piece = 1 + half
            add(None, clip_edge.at[n], edge_in.at[tm, side, piece], edge_sem.at[tm, side, piece], at, band)
        for at in range(TILES):
            add(None, clip_in.at[:, :, at * wide:(at + 1) * wide],
                own_in.at[pl.ds(tm * frames, frames), pl.ds(pair * half, pair)],
                own_sem.at[tm, half], at, band)
        return copies

    @pl.when(sender)
    def _():
        for condition, copy in clip_copies():
            when(condition, copy.start)

    def next_copies(unit, first, count):
        copies = []
        for n, (t, b) in enumerate(steps):
            if t:
                side, piece = (1 if t < 0 else 0), {-1: 3, 0: 1, 1: 0}[b]
                source = edge_out.at[unit, 1 - side]
                target, arrived = edge_in.at[unit, side, piece], edge_sem.at[unit, side, piece]
            elif b:
                source = tile_out.at[pl.ds(first, count), 0 if b < 0 else TALL - 1]
                above = 1 if b < 0 else 0
                target, arrived = row_in.at[above, pl.ds(first, count)], row_sem.at[unit, above]
            else:
                source, target = tile_out.at[pl.ds(first, count)], own_in.at[pl.ds(first, count)]
                arrived = own_sem.at[unit, 0]
            copies.append((inside(t, b), pltpu.make_async_remote_copy(
                src_ref=source,
                dst_ref=target,
                send_sem=next_send.at[unit, n],
                recv_sem=arrived,
                device_id=worker_device(section + 1, tile + t, band + b),
                device_id_type=MESH,
            )))
        return copies

    def home_copy(unit, first, count, slot, near, remote):
        source = tile_out.at[pl.ds(first, count), near * pair:(near + 1) * pair]
        target = out.at[0, slot:slot + count, :, pl.ds(pl.multiple_of(tile * wide, wide), wide)]
        if not remote:
            return pltpu.make_async_copy(source, target, home_sem.at[tile, slot])
        return pltpu.make_async_remote_copy(
            src_ref=source,
            dst_ref=target,
            send_sem=home_send.at[unit, near],
            recv_sem=home_sem.at[tile, slot],
            device_id=(section, jnp.minimum(unit, last_group), 2 * band + near),
            device_id_type=MESH,
        )

    def stays(unit, near):
        return (jnp.minimum(unit, last_group) == tm) & (near == half)

    def arrived(ref, sem):
        pltpu.make_async_copy(ref, ref, sem).wait()

    def activated(value):
        factor = lax.rsqrt(jnp.mean(value * value, axis=-1, keepdims=True) + 1e-06)
        value = value * factor * gain[...]
        return value / (1.0 + jnp.exp(-value))

    def taps(first, count, time_tap):
        summed = jnp.zeros((count * cells, channels), jnp.float32)
        for row_tap in range(TAPS):
            window = hidden[pl.ds(first + ahead, count), row_tap:row_tap + TALL]
            summed = summed + jnp.dot(
                window.reshape(count * cells, TAPS * channels),
                filters[TAPS * time_tap + row_tap],
                preferred_element_type=jnp.float32,
            )
        return summed

    def receive(unit, first, count):
        for side, t in ((0, -1), (1, 1)):
            for piece, b in ((0, -1), (1, 0), (3, 1)):
                when(inside(t, b), lambda side=side, piece=piece: arrived(
                    edge_in.at[unit, side, piece], edge_sem.at[unit, side, piece]))
        for above, b in ((0, -1), (1, 1)):
            when(inside(0, b), lambda above=above: arrived(
                row_in.at[above, pl.ds(first, count)], row_sem.at[unit, above]))

    def receive_clip(unit, first):
        for side, t in ((0, -1), (1, 1)):
            @pl.when(inside(t, 0))
            def _(side=side):
                arrived(edge_in.at[unit, side, 2], edge_sem.at[unit, side, 2])
        for near in range(2):
            arrived(own_in.at[pl.ds(first, frames), near * pair:(near + 1) * pair], own_sem.at[unit, near])

    def process(unit, first, count, slot):
        @pl.when(section > 0)
        def _():
            receive(unit, first, count)
            arrived(own_in.at[pl.ds(first, count)], own_sem.at[unit, 0])

        if slot == 0:
            @pl.when(section == 0)
            def _():
                receive(unit, first, frames)
                receive_clip(unit, first)

        at_edge = unit if slot == 0 else jnp.where(section == 0, unit - slot, unit)

        lower = lax.broadcasted_iota(jnp.int32, (edge_cells, channels), 0) >= edge_cells // 2
        pieces = []
        for side in range(2):
            above, middle, under, below = (
                jnp.concatenate(
                    [edge_in[at_edge, side, p][n * edge_cells:(n + 1) * edge_cells].astype(jnp.float32)
                     for n in range(channels // LANES)],
                    axis=1,
                )
                for p in range(4)
            )
            pieces += [above, jnp.where(lower & (section == 0), under, middle), below]
        halo[...] = activated(jnp.concatenate(pieces, axis=0))

        own = own_in[pl.ds(first, count)].reshape(count * cells, channels).astype(jnp.float32)
        middle = activated(own).reshape(count, TALL, wide, channels)
        outer = row_in[:, pl.ds(first, count)].reshape(2 * count * wide, channels).astype(jnp.float32)
        outer = activated(outer).reshape(2, count, wide, channels)
        column = lax.broadcasted_iota(jnp.int32, (wide, channels), 0)
        for n in range(count):
            frame = slot + n
            for row in range(TALL + 2):
                if row == 0:
                    here, at = outer[0, n], edge_cells // 2 + pair * frame + pair - 1
                elif row == TALL + 1:
                    here, at = outer[1, n], 2 * edge_cells + pair * frame
                else:
                    part, within = divmod(row - 1, pair)
                    here = middle[n, row - 1]
                    at = edge_cells + part * (edge_cells // 2) + pair * frame + within
                left = jnp.where(column == 0, halo[pl.ds(at, 1), :], pltpu.roll(here, 1, 0))
                at += TAPS * edge_cells
                right = jnp.where(column == wide - 1, halo[pl.ds(at, 1), :], pltpu.roll(here, wide - 1, 0))
                for part, shifted in enumerate((left, here, right)):
                    hidden[first + ahead + n, row, :, part * channels:(part + 1) * channels] = (
                        shifted.astype(jnp.bfloat16)
                    )

        if count > 1:
            @pl.when(unit == 0)
            def _():
                load_filters.wait()

        summed = partial[slot * cells:(slot + count) * cells]
        for time_tap in range(1 if count > 1 else ahead, TAPS):
            summed = summed + taps(first + time_tap - ahead, count, time_tap)
        result = own + summed
        tile_out[pl.ds(first, count)] = result.astype(jnp.bfloat16).reshape(count, TALL, wide, channels)

        @pl.when(section < sections - 1)
        def _():
            block = pair * wide
            for n in range(count):
                for part in range(TALL // pair):
                    source = (n * (TALL // pair) + part) * block
                    for lane in range(channels // LANES):
                        wide_out[lane, pl.ds((part * frames + slot + n) * block, block), :] = (
                            result[source:source + block, lane * LANES:(lane + 1) * LANES]
                        )
            for side, at in enumerate((0, wide - 1)):
                parts = [
                    wide_out[lane, pl.ds(at, edge_cells, stride=wide), :]
                    for lane in range(channels // LANES)
                ]
                edge_out[unit, side] = jnp.concatenate(parts, axis=0).astype(jnp.bfloat16)
            for condition, copy in next_copies(unit, first, count):
                when(condition, copy.start)

        for near in range(2):
            @pl.when(stays(unit, near))
            def _(near=near):
                home_copy(unit, first, count, slot, near, False).start()

            @pl.when(jnp.logical_not(stays(unit, near)))
            def _(near=near):
                home_copy(unit, first, count, slot, near, True).start()

    def process_group(unit, carry):
        process(unit, unit * frames, frames, 0)
        partial[...] = taps(unit * frames, frames, 0)
        return carry

    @pl.when(worker)
    def _():
        load_gain.wait()
        lax.fori_loop(0, last_group, process_group, 0)
        for slot in range(frames):
            frame = last_group * frames + slot
            for time_tap in range(1, ahead):
                partial[slot * cells:(slot + 1) * cells] += taps(frame + time_tap - ahead, 1, time_tap)
            process(last_group + slot, frame, 1, slot)

    @pl.when(tm < last_group)
    def _():
        for at in range(TILES):
            arrived(out.at[0, :, :, at * wide:(at + 1) * wide], home_sem.at[at, 0])

    @pl.when(tm == last_group)
    def _():
        for slot in range(frames):
            for at in range(TILES):
                arrived(out.at[0, slot:slot + 1, :, at * wide:(at + 1) * wide], home_sem.at[at, slot])

    @pl.when(sender)
    def _():
        for condition, copy in clip_copies():
            when(condition, copy.wait_send)

    def drain(unit, first, count, slot):
        @pl.when(section < sections - 1)
        def _():
            for condition, copy in next_copies(unit, first, count):
                when(condition, copy.wait_send)

        for near in range(2):
            @pl.when(jnp.logical_not(stays(unit, near)))
            def _(near=near):
                home_copy(unit, first, count, slot, near, True).wait_send()

    def drain_group(unit, carry):
        drain(unit, unit * frames, frames, 0)
        return carry

    @pl.when(worker)
    def _():
        lax.fori_loop(0, last_group, drain_group, 0)
        for slot in range(frames):
            drain(last_group + slot, last_group * frames + slot, 1, slot)


def on_device(clip_features, conv_kernels, norm_gains):
    frames, pair, columns, channels = clip_features.shape
    groups = lax.axis_size("tm")
    total = groups * frames
    units = groups - 1 + frames
    wide = columns // TILES
    edge_cells = frames * TALL
    edge = (edge_cells * channels // LANES, LANES)
    edges = 2 * (TILES - 1)
    in_hbm = pl.BlockSpec(memory_space=pltpu.HBM)
    return pl.pallas_call(
        chain_kernel,
        out_shape=jax.ShapeDtypeStruct((1, frames, pair, columns, channels), jnp.bfloat16),
        in_specs=[in_hbm] * 3,
        out_specs=in_hbm,
        scratch_shapes=[
            pltpu.VMEM((total, TALL, wide, channels), jnp.bfloat16),
            pltpu.VMEM((2, total, wide, channels), jnp.bfloat16),
            pltpu.VMEM((units, 2, 4, *edge), jnp.bfloat16),
            pltpu.VMEM((TAPS - 1 + total, TALL + 2, wide, TAPS * channels), jnp.bfloat16),
            pltpu.VMEM((frames * TALL * wide, channels), jnp.float32),
            pltpu.VMEM((2 * TAPS * edge_cells, channels), jnp.float32),
            pltpu.VMEM(conv_kernels.shape[1:], jnp.bfloat16),
            pltpu.VMEM(norm_gains.shape, jnp.float32),
            pltpu.VMEM((channels // LANES, frames * TALL * wide, LANES), jnp.float32),
            pltpu.VMEM((total, TALL, wide, channels), jnp.bfloat16),
            pltpu.VMEM((units, 2, *edge), jnp.bfloat16),
            pltpu.VMEM((frames, pair, columns, channels), jnp.bfloat16),
            pltpu.VMEM((channels // LANES, frames * pair * columns, LANES), jnp.float32),
            pltpu.VMEM((edges, *edge), jnp.bfloat16),
            pltpu.SemaphoreType.DMA((units, 2)),
            pltpu.SemaphoreType.DMA((units, 2)),
            pltpu.SemaphoreType.DMA((units, 2, 4)),
            pltpu.SemaphoreType.DMA((TILES, frames)),
            pltpu.SemaphoreType.DMA((2 * edges + 2 * TILES,)),
            pltpu.SemaphoreType.DMA((units, 9)),
            pltpu.SemaphoreType.DMA((units, 2)),
            pltpu.SemaphoreType.DMA((3,)),
        ],
        compiler_params=pltpu.CompilerParams(
            collective_id=0, has_side_effects=True, vmem_limit_bytes=56 * 2**20
        ),
        name="chain",
    )(clip_features, conv_kernels, norm_gains)


def solution(mesh):
    return jax.shard_map(
        on_device,
        mesh=mesh,
        in_specs=(P("tm", "space", None, None), P("section", None, None, None), P("section", None)),
        out_specs=P("section", "tm", "space", None, None),
        check_vma=False,
    )
```

time: 32.4 us -> 34.4 us (1.062)
  Pallas kernels: 30.7 us -> 32.7 us
    pallas_call x1, Pallas kernels: 30.7 us -> 32.7 us  [on_device(): pl.pallas_call(chain_kernel, out_shape=jax.ShapeDtypeStruct((1, frames, p...]
where the time goes in v5:
time: 34.4 us; the launch traced here: 34.3 us
  Pallas kernels  32.7 us (95%)
  local copies, waits for them, and re-layouts  1.57 us (5%)
    pallas_call x1, Pallas kernels, on_device(): pl.pallas_call(chain_kernel, out_shape=jax.ShapeDtypeStruct((1, frames, p...  32.7 us
    unnamed x1, local copies, waits for them, and re-layouts  1.57 us

profile of v5, /device:TPU:123, one launch (start us, length us, event | category | flops | bytes accessed | tf_op | source)
XLA Modules:
  0.0 34.3 jit_solution(1854347402511323345)
XLA Ops:
  0.0 32.7 %chain.1 = bf16[1,2,2,64,256]{4,3,2,1,0:T(8,128)(2,1)} custom-call(bf16[2,2,64,256]{3,2,1,0:T(8,128)(2,1)} %clip.1, bf16[1,9,768,256]{3,2,1,0:T(8,128)(2,1)} %weights.1, f32[1,256]{1,0:T(1,128)} %gains.1), custom_call_target="tpu_custom_call" | custom-call | tf_op jit(solution)/shard_map/chain/pallas_call | solution.py:431
  32.7 1.6 %copy.5 = bf16[1,2,2,64,256]{4,3,2,1,0:T(8,128)(2,1)} copy(bf16[1,2,2,64,256]{4,3,2,1,0:T(8,128)(2,1)} %chain.1) | data formatting | bytes 262144

commit v6 on v3

--- a/solution.py
+++ b/solution.py
@@ -29,7 +29,8 @@
     half = space % 2
     tile = 2 * half + tm // 2
     worker = tm % 2 == WORKER
-    sender = section == tm % sections
+    sender = section == jnp.where(tm == 0, sections - 1, tm % sections)
+    sources = [(sections - 1 if group == 0 else group % sections, group) for group in range(groups)]
     frames, pair, columns, channels = clip.shape
     wide = columns // TILES
     cells = frames * TALL * wide
@@ -64,19 +65,19 @@
 
     @pl.when(worker & (section == 0))
     def _():
-        for group in range(groups):
+        for source, group in sources:
             for near in range(2):
-                greet((group % sections, group, 2 * band + near))
+                greet((source, group, 2 * band + near))
 
         @pl.when(band > 0)
         def _():
-            for group in range(groups):
-                greet((group % sections, group, jnp.maximum(2 * band - 1, 0)))
+            for source, group in sources:
+                greet((source, group, jnp.maximum(2 * band - 1, 0)))
 
         @pl.when(band < bands - 1)
         def _():
-            for group in range(groups):
-                greet((group % sections, group, jnp.minimum(2 * band + 2, 2 * bands - 1)))
+            for source, group in sources:
+                greet((source, group, jnp.minimum(2 * band + 2, 2 * bands - 1)))
 
     load_filters = pltpu.make_async_copy(weights.at[0], filters, load_sem.at[0])
     load_gain = pltpu.make_async_copy(gains, gain, load_sem.at[1])
@@ -176,13 +177,13 @@
             piece = 3 * (1 - half)
             add(has_beside, clip_edge.at[n], edge_in.at[tm, side, piece], edge_sem.at[tm, side, piece], at, beside)
         for at in range(TILES):
-            add(has_beside, clip.at[:, half, at * wide:(at + 1) * wide], row_in.at[tm, 1 - half],
+            add(has_beside, clip_in.at[:, half, at * wide:(at + 1) * wide], row_in.at[tm, 1 - half],
                 row_sem.at[tm, 1 - half], at, beside)
         for n, (side, at, _) in enumerate(clip_edges):
             piece = 1 + half
             add(None, clip_edge.at[n], edge_in.at[tm, side, piece], edge_sem.at[tm, side, piece], at, band)
         for at in range(TILES):
-            add(None, clip.at[:, :, at * wide:(at + 1) * wide], own_in.at[tm, :, pl.ds(pair * half, pair)],
+            add(None, clip_in.at[:, :, at * wide:(at + 1) * wide], own_in.at[tm, :, pl.ds(pair * half, pair)],
                 own_sem.at[tm, half], at, band)
         return copies
 

time: 32.4 us -> 35.1 us (1.083)
  Pallas kernels: 30.7 us -> 33.4 us
    pallas_call x1, Pallas kernels: 30.7 us -> 33.4 us  [on_device(): pl.pallas_call(chain_kernel, out_shape=jax.ShapeDtypeStruct((1, frames, p...]
where the time goes in v6:
time: 35.1 us; the launch traced here: 35 us
  Pallas kernels  33.4 us (95%)
  local copies, waits for them, and re-layouts  1.57 us (4%)
    pallas_call x1, Pallas kernels, on_device(): pl.pallas_call(chain_kernel, out_shape=jax.ShapeDtypeStruct((1, frames, p...  33.4 us
    unnamed x1, local copies, waits for them, and re-layouts  1.57 us

profile of v6, /device:TPU:123, one launch (start us, length us, event | category | flops | bytes accessed | tf_op | source)
XLA Modules:
  0.0 35.0 jit_solution(15318472265011642088)
XLA Ops:
  0.0 33.4 %chain.1 = bf16[1,2,2,64,256]{4,3,2,1,0:T(8,128)(2,1)} custom-call(bf16[2,2,64,256]{3,2,1,0:T(8,128)(2,1)} %clip.1, bf16[1,9,768,256]{3,2,1,0:T(8,128)(2,1)} %weights.1, f32[1,256]{1,0:T(1,128)} %gains.1), custom_call_target="tpu_custom_call" | custom-call | tf_op jit(solution)/shard_map/chain/pallas_call | solution.py:391
  33.4 1.6 %copy.5 = bf16[1,2,2,64,256]{4,3,2,1,0:T(8,128)(2,1)} copy(bf16[1,2,2,64,256]{4,3,2,1,0:T(8,128)(2,1)} %chain.1) | data formatting | bytes 262144

commit v7 on v3

--- a/solution.py
+++ b/solution.py
@@ -15,9 +15,9 @@
 
 def chain_kernel(
     clip, weights, gains, out,
-    own_in, row_in, edge_in, hidden, halo, filters, gain, wide_out, tile_out, edge_out,
-    clip_in, clip_wide, clip_edge,
-    own_sem, row_sem, edge_sem, home_sem, clip_send, next_send, home_send, load_sem,
+    own_in, row_in, edge_in, corner_in, hidden, partial, raw, halo, filters, gain, wide_out, tile_out, edge_out,
+    corner_out, clip_in, clip_wide, clip_edge, clip_corner,
+    own_sem, row_sem, edge_sem, corner_sem, home_sem, clip_send, next_send, home_send, load_sem,
 ):
     section = lax.axis_index("section")
     tm = lax.axis_index("tm")
@@ -34,6 +34,7 @@
     wide = columns // TILES
     cells = frames * TALL * wide
     edge_cells = frames * TALL
+    ahead = TAPS - 1
     beside = band + 2 * half - 1
     has_beside = (beside >= 0) & (beside < bands)
 
@@ -105,29 +106,32 @@
 
     @pl.when(worker)
     def _():
-        hidden[0:frames] = jnp.zeros((frames, *hidden.shape[1:]), hidden.dtype)
+        hidden[0:ahead] = jnp.zeros((ahead, *hidden.shape[1:]), hidden.dtype)
+        partial[...] = jnp.zeros_like(partial)
 
         @pl.when(band == 0)
         def _():
             row_in[:, 0] = jnp.zeros((groups, *row_in.shape[2:]), row_in.dtype)
-            edge_in[:, :, 0] = jnp.zeros((groups, 2, *edge_in.shape[3:]), edge_in.dtype)
+            corner_in[:, :, 0] = jnp.zeros((groups, 2, *corner_in.shape[3:]), corner_in.dtype)
 
         @pl.when(band == bands - 1)
         def _():
             row_in[:, 1] = jnp.zeros((groups, *row_in.shape[2:]), row_in.dtype)
-            edge_in[:, :, 3] = jnp.zeros((groups, 2, *edge_in.shape[3:]), edge_in.dtype)
+            corner_in[:, :, 1] = jnp.zeros((groups, 2, *corner_in.shape[3:]), corner_in.dtype)
 
         @pl.when(section > 0)
         def _():
-            edge_in[:, :, 2] = jnp.zeros((groups, 2, *edge_in.shape[3:]), edge_in.dtype)
+            edge_in[:, :, 1] = jnp.zeros((groups, 2, *edge_in.shape[3:]), edge_in.dtype)
 
         @pl.when(tile == 0)
         def _():
             edge_in[:, 0] = jnp.zeros((groups, *edge_in.shape[2:]), edge_in.dtype)
+            corner_in[:, 0] = jnp.zeros((groups, *corner_in.shape[2:]), corner_in.dtype)
 
         @pl.when(tile == TILES - 1)
         def _():
             edge_in[:, 1] = jnp.zeros((groups, *edge_in.shape[2:]), edge_in.dtype)
+            corner_in[:, 1] = jnp.zeros((groups, *corner_in.shape[2:]), corner_in.dtype)
 
     left_edges = [(0, at, at * wide - 1) for at in range(1, TILES)]
     right_edges = [(1, at, at * wide + wide) for at in range(TILES - 1)]
@@ -144,6 +148,13 @@
                 part = clip_wide[lane, pl.ds(column, frames * pair, stride=columns), :]
                 parts += [part, part]
             clip_edge[n] = jnp.concatenate(parts, axis=0).astype(jnp.bfloat16)
+            for lane in range(channels // LANES):
+                for row in range(pair):
+                    @pl.when(half == row)
+                    def _(n=n, column=column, lane=lane, row=row):
+                        clip_corner[n, lane * frames:(lane + 1) * frames] = (
+                            clip_wide[lane, pl.ds(row * columns + column, frames, stride=pair * columns), :]
+                        )
 
     def one_if(condition):
         return jnp.where(condition, 1, 0)
@@ -173,14 +184,13 @@
             )))
 
         for n, (side, at, _) in enumerate(clip_edges):
-            piece = 3 * (1 - half)
-            add(has_beside, clip_edge.at[n], edge_in.at[tm, side, piece], edge_sem.at[tm, side, piece], at, beside)
+            add(has_beside, clip_corner.at[n], corner_in.at[tm, side, 1 - half], corner_sem.at[tm, side, 1 - half],
+                at, beside)
         for at in range(TILES):
             add(has_beside, clip.at[:, half, at * wide:(at + 1) * wide], row_in.at[tm, 1 - half],
                 row_sem.at[tm, 1 - half], at, beside)
         for n, (side, at, _) in enumerate(clip_edges):
-            piece = 1 + half
-            add(None, clip_edge.at[n], edge_in.at[tm, side, piece], edge_sem.at[tm, side, piece], at, band)
+            add(None, clip_edge.at[n], edge_in.at[tm, side, half], edge_sem.at[tm, side, half], at, band)
         for at in range(TILES):
             add(None, clip.at[:, :, at * wide:(at + 1) * wide], own_in.at[tm, :, pl.ds(pair * half, pair)],
                 own_sem.at[tm, half], at, band)
@@ -194,10 +204,14 @@
     def next_copies(group):
         copies = []
         for n, (t, b) in enumerate(steps):
-            if t:
-                side, piece = (1 if t < 0 else 0), {-1: 3, 0: 1, 1: 0}[b]
+            if t and b:
+                side, above = (1 if t < 0 else 0), (1 if b < 0 else 0)
+                source = corner_out.at[group, 1 - side, 1 - above]
+                target, arrived = corner_in.at[group, side, above], corner_sem.at[group, side, above]
+            elif t:
+                side = 1 if t < 0 else 0
                 source = edge_out.at[group, 1 - side]
-                target, arrived = edge_in.at[group, side, piece], edge_sem.at[group, side, piece]
+                target, arrived = edge_in.at[group, side, 0], edge_sem.at[group, side, 0]
             elif b:
                 source = tile_out.at[group, :, 0 if b < 0 else TALL - 1]
                 above = 1 if b < 0 else 0
@@ -237,19 +251,32 @@
     def activated(value):
         factor = lax.rsqrt(jnp.mean(value * value, axis=-1, keepdims=True) + 1e-06)
         value = value * factor * gain[...]
-        return value / (1.0 + jnp.exp(-value))
+        value = 0.5 * value
+        return value + value * jnp.tanh(value)
+
+    def taps(frame, time_tap):
+        summed = jnp.zeros((cells, channels), jnp.float32)
+        for row_tap in range(TAPS):
+            window = hidden[pl.ds(frame, frames), row_tap:row_tap + TALL]
+            summed = summed + jnp.dot(
+                window.reshape(cells, TAPS * channels),
+                filters[TAPS * time_tap + row_tap],
+                preferred_element_type=jnp.float32,
+            )
+        return summed
 
     def process(group, carry):
         first = group * frames
 
         for side, t in ((0, -1), (1, 1)):
-            for piece, b in ((0, -1), (1, 0), (3, 1)):
-                when(inside(t, b), lambda side=side, piece=piece: arrived(
-                    edge_in.at[group, side, piece], edge_sem.at[group, side, piece]))
+            for above, b in ((0, -1), (1, 1)):
+                when(inside(t, b), lambda side=side, above=above: arrived(
+                    corner_in.at[group, side, above], corner_sem.at[group, side, above]))
+            when(inside(t, 0), lambda side=side: arrived(edge_in.at[group, side, 0], edge_sem.at[group, side, 0]))
 
             @pl.when((section == 0) & inside(t, 0))
             def _(side=side):
-                arrived(edge_in.at[group, side, 2], edge_sem.at[group, side, 2])
+                arrived(edge_in.at[group, side, 1], edge_sem.at[group, side, 1])
 
         for above, b in ((0, -1), (1, 1)):
             when(inside(0, b), lambda above=above: arrived(row_in.at[group, above], row_sem.at[group, above]))
@@ -264,18 +291,24 @@
             arrived(own_in.at[group], own_sem.at[group, 0])
 
         lower = lax.broadcasted_iota(jnp.int32, (edge_cells, channels), 0) >= edge_cells // 2
-        pieces = []
+        stored = edge_cells + 2 * frames
         for side in range(2):
-            above, middle, under, below = (
+            upper, under = (
                 jnp.concatenate(
                     [edge_in[group, side, p][n * edge_cells:(n + 1) * edge_cells].astype(jnp.float32)
                      for n in range(channels // LANES)],
                     axis=1,
                 )
-                for p in range(4)
+                for p in range(2)
             )
-            pieces += [above, jnp.where(lower & (section == 0), under, middle), below]
-        halo[...] = activated(jnp.concatenate(pieces, axis=0))
+            raw[pl.ds(side * stored, edge_cells), :] = jnp.where(lower & (section == 0), under, upper)
+            for above in range(2):
+                at = side * stored + edge_cells + above * frames
+                for n in range(channels // LANES):
+                    raw[pl.ds(at, frames), n * LANES:(n + 1) * LANES] = (
+                        corner_in[group, side, above, n * frames:(n + 1) * frames]
+                    )
+        halo[...] = activated(raw[...])
 
         own = own_in[group].reshape(cells, channels).astype(jnp.float32)
         middle = activated(own).reshape(frames, TALL, wide, channels)
@@ -285,18 +318,18 @@
         for frame in range(frames):
             for row in range(TALL + 2):
                 if row == 0:
-                    here, at = outer[0, frame], edge_cells // 2 + pair * frame + pair - 1
+                    here, at = outer[0, frame], edge_cells + frame
                 elif row == TALL + 1:
-                    here, at = outer[1, frame], 2 * edge_cells + pair * frame
+                    here, at = outer[1, frame], edge_cells + frames + frame
                 else:
                     part, within = divmod(row - 1, pair)
                     here = middle[frame, row - 1]
-                    at = edge_cells + part * (edge_cells // 2) + pair * frame + within
+                    at = part * (edge_cells // 2) + pair * frame + within
                 left = jnp.where(column == 0, halo[pl.ds(at, 1), :], pltpu.roll(here, 1, 0))
-                at += TAPS * edge_cells
+                at += stored
                 right = jnp.where(column == wide - 1, halo[pl.ds(at, 1), :], pltpu.roll(here, wide - 1, 0))
                 for part, shifted in enumerate((left, here, right)):
-                    hidden[first + frames + frame, row, :, part * channels:(part + 1) * channels] = (
+                    hidden[first + ahead + frame, row, :, part * channels:(part + 1) * channels] = (
                         shifted.astype(jnp.bfloat16)
                     )
 
@@ -304,15 +337,9 @@
         def _():
             load_filters.wait()
 
-        summed = jnp.zeros((cells, channels), jnp.float32)
-        for time_tap in range(TAPS):
-            for row_tap in range(TAPS):
-                window = hidden[pl.ds(first + frames - 2 + time_tap, frames), row_tap:row_tap + TALL]
-                summed = summed + jnp.dot(
-                    window.reshape(cells, TAPS * channels),
-                    filters[TAPS * time_tap + row_tap],
-                    preferred_element_type=jnp.float32,
-                )
+        summed = partial[...]
+        for time_tap in range(1, TAPS):
+            summed = summed + taps(first + time_tap, time_tap)
         result = own + summed
         tile_out[group] = result.astype(jnp.bfloat16).reshape(frames, TALL, wide, channels)
 
@@ -332,6 +359,12 @@
                     for n in range(channels // LANES)
                 ]
                 edge_out[group, side] = jnp.concatenate(parts, axis=0).astype(jnp.bfloat16)
+                for above, start in enumerate((0, frames * block + (pair - 1) * wide)):
+                    for lane in range(channels // LANES):
+                        corner_out[group, side, above, lane * frames:(lane + 1) * frames] = (
+                            wide_out[lane, pl.ds(start + at, frames, stride=block), :]
+                            .astype(jnp.bfloat16).astype(jnp.float32)
+                        )
             for condition, copy in next_copies(group):
                 when(condition, copy.start)
 
@@ -345,6 +378,10 @@
             @pl.when(jnp.logical_not(own_home))
             def _(near=near):
                 home_copy(group, near).start()
+
+        @pl.when(group < groups - 1)
+        def _():
+            partial[...] = taps(first + frames, 0)
 
         return carry
 
@@ -385,6 +422,7 @@
     wide = columns // TILES
     edge_cells = frames * TALL
     edge = (edge_cells * channels // LANES, LANES)
+    corner = (frames * channels // LANES, LANES)
     edges = 2 * (TILES - 1)
     in_hbm = pl.BlockSpec(memory_space=pltpu.HBM)
     return pl.pallas_call(
@@ -395,20 +433,26 @@
         scratch_shapes=[
             pltpu.VMEM((groups, frames, TALL, wide, channels), jnp.bfloat16),
             pltpu.VMEM((groups, 2, frames, wide, channels), jnp.bfloat16),
-            pltpu.VMEM((groups, 2, 4, *edge), jnp.bfloat16),
-            pltpu.VMEM(((groups + 1) * frames, TALL + 2, wide, TAPS * channels), jnp.bfloat16),
-            pltpu.VMEM((2 * TAPS * edge_cells, channels), jnp.float32),
+            pltpu.VMEM((groups, 2, 2, *edge), jnp.bfloat16),
+            pltpu.VMEM((groups, 2, 2, *corner), jnp.float32),
+            pltpu.VMEM((TAPS - 1 + groups * frames, TALL + 2, wide, TAPS * channels), jnp.bfloat16),
+            pltpu.VMEM((frames * TALL * wide, channels), jnp.float32),
+            pltpu.VMEM((2 * (edge_cells + 2 * frames), channels), jnp.float32),
+            pltpu.VMEM((2 * (edge_cells + 2 * frames), channels), jnp.float32),
             pltpu.VMEM(conv_kernels.shape[1:], jnp.bfloat16),
             pltpu.VMEM(norm_gains.shape, jnp.float32),
             pltpu.VMEM((channels // LANES, frames * TALL * wide, LANES), jnp.float32),
             pltpu.VMEM((groups, frames, TALL, wide, channels), jnp.bfloat16),
             pltpu.VMEM((groups, 2, *edge), jnp.bfloat16),
+            pltpu.VMEM((groups, 2, 2, *corner), jnp.float32),
             pltpu.VMEM((frames, pair, columns, channels), jnp.bfloat16),
             pltpu.VMEM((channels // LANES, frames * pair * columns, LANES), jnp.float32),
             pltpu.VMEM((edges, *edge), jnp.bfloat16),
+            pltpu.VMEM((edges, *corner), jnp.float32),
             pltpu.SemaphoreType.DMA((groups, 2)),
             pltpu.SemaphoreType.DMA((groups, 2)),
-            pltpu.SemaphoreType.DMA((groups, 2, 4)),
+            pltpu.SemaphoreType.DMA((groups, 2, 2)),
+            pltpu.SemaphoreType.DMA((groups, 2, 2)),
             pltpu.SemaphoreType.DMA((TILES,)),
             pltpu.SemaphoreType.DMA((2 * edges + 2 * TILES,)),
             pltpu.SemaphoreType.DMA((groups, 9)),

time: 32.4 us -> 31.7 us (0.978)
  Pallas kernels: 30.7 us -> 30 us
    pallas_call x1, Pallas kernels: 30.7 us -> 30 us  [on_device(): pl.pallas_call(chain_kernel, out_shape=jax.ShapeDtypeStruct((1, frames, p...]
where the time goes in v7:
time: 31.7 us; the launch traced here: 31.6 us
  Pallas kernels  30 us (95%)
  local copies, waits for them, and re-layouts  1.57 us (5%)
    pallas_call x1, Pallas kernels, on_device(): pl.pallas_call(chain_kernel, out_shape=jax.ShapeDtypeStruct((1, frames, p...  30 us
    unnamed x1, local copies, waits for them, and re-layouts  1.57 us

profile of v7, /device:TPU:123, one launch (start us, length us, event | category | flops | bytes accessed | tf_op | source)
XLA Modules:
  0.0 31.6 jit_solution(10593013837345645665)
XLA Ops:
  0.0 30.0 %chain.1 = bf16[1,2,2,64,256]{4,3,2,1,0:T(8,128)(2,1)} custom-call(bf16[2,2,64,256]{3,2,1,0:T(8,128)(2,1)} %clip.1, bf16[1,9,768,256]{3,2,1,0:T(8,128)(2,1)} %weights.1, f32[1,256]{1,0:T(1,128)} %gains.1), custom_call_target="tpu_custom_call" | custom-call | tf_op jit(solution)/shard_map/chain/pallas_call | solution.py:428
  30.0 1.6 %copy.5 = bf16[1,2,2,64,256]{4,3,2,1,0:T(8,128)(2,1)} copy(bf16[1,2,2,64,256]{4,3,2,1,0:T(8,128)(2,1)} %chain.1) | data formatting | bytes 262144

commit v8 on v7

--- a/solution.py
+++ b/solution.py
@@ -27,7 +27,8 @@
     bands = lax.axis_size("space") // 2
     band = space // 2
     half = space % 2
-    tile = 2 * half + tm // 2
+    run = tm // 2
+    tile = 2 * half + run
     worker = tm % 2 == WORKER
     sender = section == tm % sections
     frames, pair, columns, channels = clip.shape
@@ -38,11 +39,19 @@
     beside = band + 2 * half - 1
     has_beside = (beside >= 0) & (beside < bands)
 
-    def worker_device(at_section, at_tile, at_band):
-        at_section = jnp.clip(at_section, 0, sections - 1)
-        at_tile = jnp.clip(at_tile, 0, TILES - 1)
-        at_band = jnp.clip(at_band, 0, bands - 1)
-        return (at_section, 2 * (at_tile % 2) + WORKER, 2 * at_band + at_tile // 2)
+    near_tm = {0: 2 * run + WORKER, 1: 2 * (1 - run) + WORKER, -1: 2 * (1 - run) + WORKER}
+    near_half = {0: half, 1: jnp.minimum(half + run, 1), -1: jnp.maximum(half + run - 1, 0)}
+    near_band = {0: 2 * band, 1: 2 * jnp.minimum(band + 1, bands - 1), -1: 2 * jnp.maximum(band - 1, 0)}
+    near_space = {(t, b): near_band[b] + near_half[t] for t in (-1, 0, 1) for b in (-1, 0, 1)}
+    next_section = jnp.minimum(section + 1, sections - 1)
+    previous_section = jnp.maximum(section - 1, 0)
+    beside_space = 2 * jnp.clip(beside, 0, bands - 1)
+
+    def neighbour(at_section, t, b):
+        return (at_section, near_tm[t], near_space[t, b])
+
+    def in_band(at_section, at_tile, at_space):
+        return (at_section, 2 * (at_tile % 2) + WORKER, at_space + at_tile // 2)
 
     def inside(step_tile, step_band):
         there = None
@@ -97,12 +106,12 @@
     @pl.when(worker & (section > 0))
     def _():
         for t, b in steps:
-            when(inside(t, b), lambda t=t, b=b: greet(worker_device(section - 1, tile + t, band + b)))
+            when(inside(t, b), lambda t=t, b=b: greet(neighbour(previous_section, t, b)))
 
     for near in range(TILES):
         @pl.when(jnp.logical_not(worker & (tile == near)))
         def _(near=near):
-            greet(worker_device(section, near, band))
+            greet(in_band(section, near, near_band[0]))
 
     @pl.when(worker)
     def _():
@@ -173,27 +182,27 @@
     def clip_copies():
         copies = []
 
-        def add(condition, source, target, arrived, at_tile, at_band):
+        def add(condition, source, target, arrived, at_tile, at_space):
             copies.append((condition, pltpu.make_async_remote_copy(
                 src_ref=source,
                 dst_ref=target,
                 send_sem=clip_send.at[len(copies)],
                 recv_sem=arrived,
-                device_id=worker_device(0, at_tile, at_band),
+                device_id=in_band(0, at_tile, at_space),
                 device_id_type=MESH,
             )))
 
         for n, (side, at, _) in enumerate(clip_edges):
             add(has_beside, clip_corner.at[n], corner_in.at[tm, side, 1 - half], corner_sem.at[tm, side, 1 - half],
-                at, beside)
+                at, beside_space)
         for at in range(TILES):
             add(has_beside, clip.at[:, half, at * wide:(at + 1) * wide], row_in.at[tm, 1 - half],
-                row_sem.at[tm, 1 - half], at, beside)
+                row_sem.at[tm, 1 - half], at, beside_space)
         for n, (side, at, _) in enumerate(clip_edges):
-            add(None, clip_edge.at[n], edge_in.at[tm, side, half], edge_sem.at[tm, side, half], at, band)
+            add(None, clip_edge.at[n], edge_in.at[tm, side, half], edge_sem.at[tm, side, half], at, near_band[0])
         for at in range(TILES):
             add(None, clip.at[:, :, at * wide:(at + 1) * wide], own_in.at[tm, :, pl.ds(pair * half, pair)],
-                own_sem.at[tm, half], at, band)
+                own_sem.at[tm, half], at, near_band[0])
         return copies
 
     @pl.when(sender)
@@ -223,7 +232,7 @@
                 dst_ref=target,
                 send_sem=next_send.at[group, n],
                 recv_sem=arrived,
-                device_id=worker_device(section + 1, tile + t, band + b),
+                device_id=neighbour(next_section, t, b),
                 device_id_type=MESH,
             )))
         return copies

time: 31.7 us -> 31.6 us (level)
  no operation moved by 1% of the time
where the time goes in v8:
time: 31.6 us; the launch traced here: 31.5 us
  Pallas kernels  29.9 us (95%)
  local copies, waits for them, and re-layouts  1.57 us (5%)
    pallas_call x1, Pallas kernels, on_device(): pl.pallas_call(chain_kernel, out_shape=jax.ShapeDtypeStruct((1, frames, p...  29.9 us
    unnamed x1, local copies, waits for them, and re-layouts  1.57 us

profile of v8, /device:TPU:123, one launch (start us, length us, event | category | flops | bytes accessed | tf_op | source)
XLA Modules:
  0.0 31.5 jit_solution(7290903795010259761)
XLA Ops:
  0.0 29.9 %chain.1 = bf16[1,2,2,64,256]{4,3,2,1,0:T(8,128)(2,1)} custom-call(bf16[2,2,64,256]{3,2,1,0:T(8,128)(2,1)} %clip.1, bf16[1,9,768,256]{3,2,1,0:T(8,128)(2,1)} %weights.1, f32[1,256]{1,0:T(1,128)} %gains.1), custom_call_target="tpu_custom_call" | custom-call | tf_op jit(solution)/shard_map/chain/pallas_call | solution.py:437
  29.9 1.6 %copy.5 = bf16[1,2,2,64,256]{4,3,2,1,0:T(8,128)(2,1)} copy(bf16[1,2,2,64,256]{4,3,2,1,0:T(8,128)(2,1)} %chain.1) | data formatting | bytes 262144

commit v9 on v3

v9 whole, which is shorter than its diff:
```python
import jax
import jax.numpy as jnp
from jax import lax
from jax.experimental import pallas as pl
from jax.experimental.pallas import tpu as pltpu
from jax.sharding import PartitionSpec as P

MESH = pl.DeviceIdType.MESH
WORKER = 1
TAPS = 3
TALL = 4
HEAD = 3
TILES = 4
LANES = 128


def chain_kernel(
    clip, weights, gains, out,
    rows_in, edge_in, hidden, partial, halo, filters, gain, wide_out, tile_out, edge_out,
    clip_in, clip_wide, clip_edge,
    rows_sem, edge_sem, home_sem, clip_send, next_send, home_send, load_sem,
):
    section = lax.axis_index("section")
    tm = lax.axis_index("tm")
    space = lax.axis_index("space")
    sections = lax.axis_size("section")
    groups = lax.axis_size("tm")
    bands = lax.axis_size("space") // 2
    band = space // 2
    half = space % 2
    run = tm // 2
    tile = 2 * half + run
    worker = tm % 2 == WORKER
    sender = section == tm % sections
    frames, pair, columns, channels = clip.shape
    wide = columns // TILES
    cells = frames * TALL * wide
    edge_cells = frames * TALL
    ahead = TAPS - 1
    low = sections - 1 - section
    first_band = band == 0
    has_below = band < bands - 1

    near_tm = {0: 2 * run + WORKER, 1: 2 * (1 - run) + WORKER, -1: 2 * (1 - run) + WORKER}
    near_half = {0: half, 1: jnp.minimum(half + run, 1), -1: jnp.maximum(half + run - 1, 0)}
    near_band = {0: 2 * band, 1: 2 * jnp.minimum(band + 1, bands - 1), -1: 2 * jnp.maximum(band - 1, 0)}
    near_space = {(t, b): near_band[b] + near_half[t] for t in (-1, 0, 1) for b in (-1, 0, 1)}
    next_section = jnp.minimum(section + 1, sections - 1)
    previous_section = jnp.maximum(section - 1, 0)

    def neighbour(at_section, t, b):
        return (at_section, near_tm[t], near_space[t, b])

    def in_band(at_section, at_tile, at_space):
        return (at_section, 2 * (at_tile % 2) + WORKER, at_space + at_tile // 2)

    def owner(row):
        return jnp.maximum(row - low, 0) // TALL

    def inside(t):
        return (tile > 0) if t < 0 else (tile < TILES - 1)

    def tile_when(t, action):
        if t:
            pl.when(inside(t))(action)
        else:
            action()

    barrier = pltpu.get_barrier_semaphore()

    def greet(device):
        pl.semaphore_signal(barrier, inc=1, device_id=device, device_id_type=MESH)

    @pl.when(worker)
    def _():
        rows_in[...] = jnp.zeros_like(rows_in)
        edge_in[...] = jnp.zeros_like(edge_in)
        hidden[0:ahead] = jnp.zeros((ahead, *hidden.shape[1:]), hidden.dtype)
        partial[...] = jnp.zeros_like(partial)

    @pl.when(worker & (section == 0))
    def _():
        for group in range(groups):
            greet((group % sections, group, near_band[0] + 1))

        @pl.when(has_below)
        def _():
            for group in range(groups):
                for near in range(2):
                    greet((group % sections, group, near_band[1] + near))

        @pl.when(first_band)
        def _():
            for group in range(groups):
                greet((group % sections, group, 0))

    load_filters = pltpu.make_async_copy(weights.at[0], filters, load_sem.at[0])
    load_gain = pltpu.make_async_copy(gains, gain, load_sem.at[1])
    load_clip = pltpu.make_async_copy(clip, clip_in, load_sem.at[2])

    @pl.when(sender)
    def _():
        load_clip.start()

    @pl.when(worker)
    def _():
        load_gain.start()
        load_filters.start()

    @pl.when(worker & (section > 0))
    def _():
        for t in (-1, 1, 0):
            def _(t=t):
                greet(neighbour(previous_section, t, 0))

                @pl.when(band > 0)
                def _():
                    greet(neighbour(previous_section, t, -1))

            tile_when(t, _)

    owners = [owner(2 * space + near) for near in range(pair)]
    for near in range(pair):
        for at in range(TILES):
            @pl.when(jnp.logical_not(worker & (tile == at) & (owners[near] == band)))
            def _(near=near, at=at):
                greet(in_band(section, at, 2 * owners[near]))

    left_edges = [(0, at, at * wide - 1) for at in range(1, TILES)]
    right_edges = [(1, at, at * wide + wide) for at in range(TILES - 1)]
    clip_edges = left_edges + right_edges

    @pl.when(sender)
    def _():
        load_clip.wait()
        for n in range(channels // LANES):
            clip_wide[n] = clip_in[:, :, :, n * LANES:(n + 1) * LANES].reshape(-1, LANES).astype(jnp.float32)
        for n, (_, _, column) in enumerate(clip_edges):
            parts = []
            for lane in range(channels // LANES):
                cells_of = [
                    clip_wide[lane, pl.ds(row * columns + column, frames, stride=pair * columns), :]
                    for row in range(pair)
                ]
                parts += cells_of + cells_of
            clip_edge[n] = jnp.concatenate(parts, axis=0).astype(jnp.bfloat16)


    def one_if(condition):
        return jnp.where(condition, 1, 0)

    near_tiles = 1 + one_if(tile > 0) + one_if(tile < TILES - 1)
    own_rows = TALL - one_if(band == bands - 1) * low + one_if(first_band) * low
    own_homes = one_if(owners[0] == band) + one_if(owners[1] == band)
    receivers = (
        one_if(sender) * TILES * (1 + one_if((half == 1) & (band > 0)))
        + one_if(worker) * (
            own_rows * groups - own_homes + one_if(section < sections - 1) * near_tiles * (1 + one_if(has_below))
        )
    )

    @pl.when(receivers > 0)
    def _():
        pl.semaphore_wait(barrier, receivers)

    def clip_copies(part, at_space, start):
        copies = []

        def add(source, target, arrived, at):
            copies.append(pltpu.make_async_remote_copy(
                src_ref=source,
                dst_ref=target,
                send_sem=clip_send.at[start + len(copies)],
                recv_sem=arrived,
                device_id=in_band(0, at, at_space),
                device_id_type=MESH,
            ))

        for n, (side, at, _) in enumerate(clip_edges):
            add(clip_edge.at[n], edge_in.at[tm, side, part], edge_sem.at[tm, side, part], at)
        for at in range(TILES):
            add(clip_in.at[:, :, at * wide:(at + 1) * wide], rows_in.at[tm, :, pl.ds(1 + 2 * part, pair)],
                rows_sem.at[tm, part], at)
        return copies

    clip_part = jnp.where(half == 1, 1, jnp.where(first_band, 0, 2))
    clip_space = jnp.where(half == 1, near_band[0], near_band[-1])

    def both_clip_copies(act):
        @pl.when(sender)
        def _():
            for copy in clip_copies(clip_part, clip_space, 0):
                act(copy)

        @pl.when(sender & (half == 1) & (band > 0))
        def _():
            for copy in clip_copies(3, near_band[-1], len(clip_edges) + TILES):
                act(copy)

    both_clip_copies(lambda copy: copy.start())

    def next_copy(group, t, part):
        step = 1 if part == 1 else 0
        if t:
            side = 1 if t < 0 else 0
            source = edge_out.at[group, 1 - side, 0 if part else 1]
            target, arrived = edge_in.at[group, side, part], edge_sem.at[group, side, part]
        else:
            begin, end = ((0, HEAD), (HEAD + TALL - 2, HEAD + TALL), (HEAD, HEAD + TALL))[part]
            source = tile_out.at[group, :, begin:end]
            offset = 2 - step * TALL
            target, arrived = rows_in.at[group, :, begin + offset:end + offset], rows_sem.at[group, part]
        return pltpu.make_async_remote_copy(
            src_ref=source,
            dst_ref=target,
            send_sem=next_send.at[group, t + 1, part],
            recv_sem=arrived,
            device_id=neighbour(next_section, t, step),
            device_id_type=MESH,
        )

    def all_next_copies(group, act):
        for part, condition in ((1, has_below), (0, first_band), (2, None)):
            def _(part=part):
                for t in (-1, 1, 0):
                    tile_when(t, lambda t=t: act(next_copy(group, t, part)))

            if condition is None:
                _()
            else:
                pl.when(condition)(_)

    def home_copy(group, row, remote):
        source = tile_out.at[group, :, HEAD + row]
        at = jnp.maximum(low + row, 0)
        within = at % TALL
        target = out.at[0, :, within % pair, pl.ds(pl.multiple_of(tile * wide, wide), wide)]
        at_space = jnp.minimum(near_band[0] + 2 * (at // TALL) + within // pair, 2 * bands - 1)
        if not remote:
            return pltpu.make_async_copy(source, target, home_sem.at[tile, within % pair]), at_space
        return pltpu.make_async_remote_copy(
            src_ref=source,
            dst_ref=target,
            send_sem=home_send.at[group, HEAD + row],
            recv_sem=home_sem.at[tile, within % pair],
            device_id=(section, group, at_space),
            device_id_type=MESH,
        ), at_space

    def all_home_copies(group, act):
        for row in range(-HEAD, TALL):
            there = (first_band & (low + row >= 0)) if row < 0 else (TALL * band + low + row < TALL * bands)

            @pl.when(there)
            def _(row=row):
                remote, at_space = home_copy(group, row, True)
                stays = (group == tm) & (at_space == space)

                @pl.when(jnp.logical_not(stays))
                def _():
                    act(remote)

                if act is start:
                    @pl.when(stays)
                    def _():
                        home_copy(group, row, False)[0].start()

    def start(copy):
        copy.start()

    def wait_send(copy):
        copy.wait_send()

    def arrived(ref, sem):
        pltpu.make_async_copy(ref, ref, sem).wait()

    def activated(value):
        factor = lax.rsqrt(jnp.mean(value * value, axis=-1, keepdims=True) + 1e-06)
        value = value * factor * gain[...]
        value = 0.5 * value
        return value + value * jnp.tanh(value)

    def taps(frame, time_tap, top):
        count = HEAD + TALL - top
        summed = jnp.zeros((frames * count * wide, channels), jnp.float32)
        for row_tap in range(TAPS):
            window = hidden[pl.ds(frame, frames), top + row_tap:top + row_tap + count]
            summed = summed + jnp.dot(
                window.reshape(frames * count * wide, TAPS * channels),
                filters[TAPS * time_tap + row_tap],
                preferred_element_type=jnp.float32,
            )
        return summed

    def receive(group, part, rows):
        for side, t in ((0, -1), (1, 1)):
            tile_when(t, lambda side=side: arrived(edge_in.at[group, side, part], edge_sem.at[group, side, part]))
        arrived(rows_in.at[group, :, rows[0]:rows[1]], rows_sem.at[group, part])

    def process(group, top):
        first = group * frames
        count = HEAD + TALL - top

        @pl.when(section == 0)
        def _():
            if top == 0:
                receive(group, 0, (1, 3))
            receive(group, 1, (3, 5))

            @pl.when(has_below)
            def _():
                receive(group, 2, (5, 7))
                receive(group, 3, (7, 9))

        @pl.when(section > 0)
        def _():
            if top == 0:
                receive(group, 0, (2, 5))
            else:
                receive(group, 1, (3, 5))
            receive(group, 2, (5, 9))

        lower = lax.broadcasted_iota(jnp.int32, (edge_cells, channels), 0) >= edge_cells // 2
        pieces = []
        for side in range(2):
            upper, above, middle, under = (
                jnp.concatenate(
                    [edge_in[group, side, p][n * edge_cells:(n + 1) * edge_cells].astype(jnp.float32)
                     for n in range(channels // LANES)],
                    axis=1,
                )
                for p in range(4)
            )
            pieces += [jnp.where(lower & (section == 0), under, middle), above] + ([upper] if top == 0 else [])
        halo[0:len(pieces) * edge_cells] = activated(jnp.concatenate(pieces, axis=0))
        per_side = len(pieces) // 2 * edge_cells

        def edge_cell(side, row, frame):
            def cell(piece, at):
                return halo[pl.ds(side * per_side + piece * edge_cells + at * frames + frame, 1), :]

            if row >= 5:
                return cell(0, row - 5)
            if top:
                return cell(1, row - 1)
            if row >= 3:
                return jnp.where(section == 0, cell(1, row - 1), cell(2, row - 2))
            if row == 2:
                return jnp.where(section == 0, cell(2, 1), cell(2, 0))
            return cell(2, 0)

        taken = count + TAPS - 1
        given = rows_in[group, :, top:top + taken].reshape(frames * taken * wide, channels).astype(jnp.float32)
        values = activated(given).reshape(frames, taken, wide, channels)
        column = lax.broadcasted_iota(jnp.int32, (wide, channels), 0)
        for frame in range(frames):
            for row in range(top, top + taken):
                here = values[frame, row - top]
                image_row = TALL * band + low - TALL + row
                inside_image = (image_row >= 0) & (image_row < TALL * bands)
                left = jnp.where(column == 0, edge_cell(0, row, frame), pltpu.roll(here, 1, 0))
                right = jnp.where(column == wide - 1, edge_cell(1, row, frame), pltpu.roll(here, wide - 1, 0))
                for part, shifted in enumerate((left, here, right)):
                    hidden[first + ahead + frame, row, :, part * channels:(part + 1) * channels] = (
                        jnp.where(inside_image, shifted, 0.0).astype(jnp.bfloat16)
                    )

        @pl.when(group == 0)
        def _():
            load_filters.wait()

        own = given.reshape(frames, taken, wide, channels)[:, 1:1 + count].reshape(frames * count * wide, channels)
        summed = partial[0:frames * count * wide]
        for time_tap in range(1, TAPS):
            summed = summed + taps(first + time_tap, time_tap, top)
        result = own + summed
        tile_out[group, :, top:] = result.astype(jnp.bfloat16).reshape(frames, count, wide, channels)

        @pl.when(section < sections - 1)
        def _():
            for frame in range(frames):
                for row in range(count):
                    source = (frame * count + row) * wide
                    at = (row + top - HEAD) if row + top >= HEAD else TALL + row
                    for lane in range(channels // LANES):
                        wide_out[lane, pl.ds((at * frames + frame) * wide, wide), :] = (
                            result[source:source + wide, lane * LANES:(lane + 1) * LANES]
                        )
            for side, at in enumerate((0, wide - 1)):
                for piece in range(1 if top else 2):
                    parts = [
                        wide_out[lane, pl.ds(piece * edge_cells * wide + at, edge_cells, stride=wide), :]
                        for lane in range(channels // LANES)
                    ]
                    edge_out[group, side, piece] = jnp.concatenate(parts, axis=0).astype(jnp.bfloat16)
            all_next_copies(group, start)

        all_home_copies(group, start)

        @pl.when(group < groups - 1)
        def _():
            partial[0:frames * count * wide] = taps(first + frames, 0, top)

    def process_group(group, carry):
        @pl.when(first_band)
        def _():
            process(group, 0)

        @pl.when(jnp.logical_not(first_band))
        def _():
            process(group, HEAD)

        return carry

    @pl.when(worker)
    def _():
        wide_out[...] = jnp.zeros_like(wide_out)
        load_gain.wait()
        lax.fori_loop(0, groups, process_group, 0)

    for near in range(pair):
        for at in range(TILES):
            arrived(out.at[0, :, near, at * wide:(at + 1) * wide], home_sem.at[at, near])

    both_clip_copies(wait_send)

    def drain(group, carry):
        @pl.when(section < sections - 1)
        def _():
            all_next_copies(group, wait_send)

        all_home_copies(group, wait_send)
        return carry

    @pl.when(worker)
    def _():
        lax.fori_loop(0, groups, drain, 0)


def on_device(clip_features, conv_kernels, norm_gains):
    frames, pair, columns, channels = clip_features.shape
    groups = lax.axis_size("tm")
    wide = columns // TILES
    edge_cells = frames * TALL
    edge = (edge_cells * channels // LANES, LANES)
    tallest = HEAD + TALL
    edges = 2 * (TILES - 1)
    in_hbm = pl.BlockSpec(memory_space=pltpu.HBM)
    return pl.pallas_call(
        chain_kernel,
        out_shape=jax.ShapeDtypeStruct((1, frames, pair, columns, channels), jnp.bfloat16),
        in_specs=[in_hbm] * 3,
        out_specs=in_hbm,
        scratch_shapes=[
            pltpu.VMEM((groups, frames, tallest + 2, wide, channels), jnp.bfloat16),
            pltpu.VMEM((groups, 2, 4, *edge), jnp.bfloat16),
            pltpu.VMEM((TAPS - 1 + groups * frames, tallest + 2, wide, TAPS * channels), jnp.bfloat16),
            pltpu.VMEM((frames * tallest * wide, channels), jnp.float32),
            pltpu.VMEM((2 * 3 * edge_cells, channels), jnp.float32),
            pltpu.VMEM(conv_kernels.shape[1:], jnp.bfloat16),
            pltpu.VMEM(norm_gains.shape, jnp.float32),
            pltpu.VMEM((channels // LANES, frames * 2 * TALL * wide, LANES), jnp.float32),
            pltpu.VMEM((groups, frames, tallest, wide, channels), jnp.bfloat16),
            pltpu.VMEM((groups, 2, 2, *edge), jnp.bfloat16),
            pltpu.VMEM((frames, pair, columns, channels), jnp.bfloat16),
            pltpu.VMEM((channels // LANES, frames * pair * columns, LANES), jnp.float32),
            pltpu.VMEM((edges, *edge), jnp.bfloat16),
            pltpu.SemaphoreType.DMA((groups, 4)),
            pltpu.SemaphoreType.DMA((groups, 2, 4)),
            pltpu.SemaphoreType.DMA((TILES, pair)),
            pltpu.SemaphoreType.DMA((2 * (edges + TILES),)),
            pltpu.SemaphoreType.DMA((groups, 3, 3)),
            pltpu.SemaphoreType.DMA((groups, tallest)),
            pltpu.SemaphoreType.DMA((3,)),
        ],
        compiler_params=pltpu.CompilerParams(
            collective_id=0, has_side_effects=True, vmem_limit_bytes=56 * 2**20
        ),
        name="chain",
    )(clip_features, conv_kernels, norm_gains)


def solution(mesh):
    return jax.shard_map(
        on_device,
        mesh=mesh,
        in_specs=(P("tm", "space", None, None), P("section", None, None, None), P("section", None)),
        out_specs=P("section", "tm", "space", None, None),
        check_vma=False,
    )
```

time: 32.4 us -> 34.8 us (1.074)
  the two profiles are of different devices: /device:TPU:123 before, /device:TPU:27 now
where the time goes in v9:
time: 34.8 us; the launch traced here: 34.7 us
  Pallas kernels  33.1 us (95%)
  local copies, waits for them, and re-layouts  1.57 us (5%)
    pallas_call x1, Pallas kernels, on_device(): pl.pallas_call(chain_kernel, out_shape=jax.ShapeDtypeStruct((1, frames, p...  33.1 us
    unnamed x1, local copies, waits for them, and re-layouts  1.57 us

profile of v9, /device:TPU:27, one launch (start us, length us, event | category | flops | bytes accessed | tf_op | source)
XLA Modules:
  0.0 34.7 jit_solution(6698311560331813851)
XLA Ops:
  0.0 33.1 %chain.1 = bf16[1,2,2,64,256]{4,3,2,1,0:T(8,128)(2,1)} custom-call(bf16[2,2,64,256]{3,2,1,0:T(8,128)(2,1)} %clip.1, bf16[1,9,768,256]{3,2,1,0:T(8,128)(2,1)} %weights.1, f32[1,256]{1,0:T(1,128)} %gains.1), custom_call_target="tpu_custom_call" | custom-call | tf_op jit(solution)/shard_map/chain/pallas_call | solution.py:449
  33.1 1.6 %copy.5 = bf16[1,2,2,64,256]{4,3,2,1,0:T(8,128)(2,1)} copy(bf16[1,2,2,64,256]{4,3,2,1,0:T(8,128)(2,1)} %chain.1) | data formatting | bytes 262144

commit v10 on v9

v10 whole, which is shorter than its diff:
```python
import jax
import jax.numpy as jnp
from jax import lax
from jax.experimental import pallas as pl
from jax.experimental.pallas import tpu as pltpu
from jax.sharding import PartitionSpec as P

MESH = pl.DeviceIdType.MESH
WORKER = 1
EXTRA_Z = 1
TAPS = 3
TALL = 4
TILES = 4
LANES = 128


def chain_kernel(
    clip, weights, gains, out,
    rows_in, edge_in, hidden, partial, halo, filters, gain, wide_out, tile_out, edge_out,
    clip_in, clip_wide, clip_edge,
    rows_sem, edge_sem, home_sem, clip_send, next_send, home_send, load_sem,
):
    section = lax.axis_index("section")
    tm = lax.axis_index("tm")
    space = lax.axis_index("space")
    sections = lax.axis_size("section")
    groups = lax.axis_size("tm")
    bands = lax.axis_size("space") // 2
    home_band = space // 2
    half = space % 2
    run = tm // 2
    tile = 2 * half + run
    extra = (tm % 2 != WORKER) & (home_band == EXTRA_Z)
    worker = (tm % 2 == WORKER) | extra
    band = jnp.where(extra, -1, home_band)
    sender = section == jnp.where((tm == 0) & (space == 0), 1, tm % sections)
    frames, pair, columns, channels = clip.shape
    wide = columns // TILES
    cells = frames * TALL * wide
    edge_cells = frames * TALL
    ahead = TAPS - 1
    low = sections - 1 - section
    has_above = band >= 0
    has_below = band < bands - 1

    def worker_device(at_section, at_tile, at_band):
        return (
            at_section,
            2 * (at_tile % 2) + jnp.where(at_band < 0, 1 - WORKER, WORKER),
            2 * jnp.where(at_band < 0, EXTRA_Z, at_band) + at_tile // 2,
        )

    near_run = {0: run, 1: 1 - run, -1: 1 - run}
    near_half = {0: half, 1: jnp.minimum(half + run, 1), -1: jnp.maximum(half + run - 1, 0)}
    near_band = {0: band, 1: jnp.minimum(band + 1, bands - 1), -1: jnp.maximum(band - 1, -1)}
    near_core = {b: jnp.where(near_band[b] < 0, 1 - WORKER, WORKER) for b in near_band}
    near_z = {b: jnp.where(near_band[b] < 0, EXTRA_Z, near_band[b]) for b in near_band}
    near_tm = {(t, b): 2 * near_run[t] + near_core[b] for t in near_run for b in near_band}
    near_space = {(t, b): 2 * near_z[b] + near_half[t] for t in near_run for b in near_band}
    next_section = jnp.minimum(section + 1, sections - 1)
    previous_section = jnp.maximum(section - 1, 0)

    def neighbour(at_section, t, b):
        return (at_section, near_tm[t, b], near_space[t, b])

    def owner(row):
        return (row - low + TALL) // TALL - 1

    homes = []
    for row in range(TALL):
        at = TALL * band + low + row
        kept = jnp.clip(at, 0, TALL * bands - 1)
        homes.append(((at >= 0) & (at < TALL * bands), kept // pair, kept % pair))

    def inside(t):
        return (tile > 0) if t < 0 else (tile < TILES - 1)

    def tile_when(t, action):
        if t:
            pl.when(inside(t))(action)
        else:
            action()

    barrier = pltpu.get_barrier_semaphore()

    def greet(device):
        pl.semaphore_signal(barrier, inc=1, device_id=device, device_id_type=MESH)

    @pl.when(worker)
    def _():
        rows_in[...] = jnp.zeros_like(rows_in)
        edge_in[...] = jnp.zeros_like(edge_in)
        hidden[0:ahead] = jnp.zeros((ahead, *hidden.shape[1:]), hidden.dtype)
        partial[...] = jnp.zeros_like(partial)

    @pl.when(worker & (section == 0))
    def _():
        @pl.when(has_below)
        def _():
            for group in range(groups):
                source = jnp.where(band < 0, 1, 0) if group == 0 else group % sections
                greet((source, group, 2 * near_band[1]))
                greet((group % sections, group, 2 * near_band[1] + 1))

        @pl.when(has_above)
        def _():
            for group in range(groups):
                greet((group % sections, group, 2 * jnp.maximum(band, 0) + 1))

    load_filters = pltpu.make_async_copy(weights.at[0], filters, load_sem.at[0])
    load_gain = pltpu.make_async_copy(gains, gain, load_sem.at[1])
    load_clip = pltpu.make_async_copy(clip, clip_in, load_sem.at[2])

    @pl.when(sender)
    def _():
        load_clip.start()

    @pl.when(worker)
    def _():
        load_gain.start()
        load_filters.start()

    @pl.when(worker & (section > 0))
    def _():
        for t in (-1, 1, 0):
            def _(t=t):
                greet(neighbour(previous_section, t, 0))

                @pl.when(has_above)
                def _():
                    greet(neighbour(previous_section, t, -1))

            tile_when(t, _)

    owners = [owner(2 * space + near) for near in range(pair)]
    for near in range(pair):
        for at in range(TILES):
            @pl.when(jnp.logical_not(worker & (tile == at) & (owners[near] == band)))
            def _(near=near, at=at):
                greet(worker_device(section, at, owners[near]))

    left_edges = [(0, at, at * wide - 1) for at in range(1, TILES)]
    right_edges = [(1, at, at * wide + wide) for at in range(TILES - 1)]
    clip_edges = left_edges + right_edges

    @pl.when(sender)
    def _():
        load_clip.wait()
        for n in range(channels // LANES):
            clip_wide[n] = clip_in[:, :, :, n * LANES:(n + 1) * LANES].reshape(-1, LANES).astype(jnp.float32)
        for n, (_, _, column) in enumerate(clip_edges):
            parts = []
            for lane in range(channels // LANES):
                cells_of = [
                    clip_wide[lane, pl.ds(row * columns + column, frames, stride=pair * columns), :]
                    for row in range(pair)
                ]
                parts += cells_of + cells_of
            clip_edge[n] = jnp.concatenate(parts, axis=0).astype(jnp.bfloat16)


    def one_if(condition):
        return jnp.where(condition, 1, 0)

    near_tiles = 1 + one_if(tile > 0) + one_if(tile < TILES - 1)
    own_rows = sum(one_if(there) for there, _, _ in homes)
    own_homes = one_if(owners[0] == band) + one_if(owners[1] == band)
    receivers = (
        one_if(sender) * TILES * (1 + half)
        + one_if(worker) * (
            own_rows * groups - own_homes + one_if(section < sections - 1) * near_tiles * (1 + one_if(has_below))
        )
    )

    @pl.when(receivers > 0)
    def _():
        pl.semaphore_wait(barrier, receivers)

    def clip_copies(part, at_band, start):
        copies = []

        def add(source, target, arrived, at):
            copies.append(pltpu.make_async_remote_copy(
                src_ref=source,
                dst_ref=target,
                send_sem=clip_send.at[start + len(copies)],
                recv_sem=arrived,
                device_id=worker_device(0, at, at_band),
                device_id_type=MESH,
            ))

        for n, (side, at, _) in enumerate(clip_edges):
            add(clip_edge.at[n], edge_in.at[tm, side, part], edge_sem.at[tm, side, part], at)
        for at in range(TILES):
            add(clip_in.at[:, :, at * wide:(at + 1) * wide], rows_in.at[tm, :, pl.ds(2 * part, pair)],
                rows_sem.at[tm, part], at)
        return copies

    def both_clip_copies(act):
        @pl.when(sender)
        def _():
            for copy in clip_copies(1 - half, home_band - 1 + half, 0):
                act(copy)

        @pl.when(sender & (half == 1))
        def _():
            for copy in clip_copies(2, home_band - 1, len(clip_edges) + TILES):
                act(copy)

    both_clip_copies(lambda copy: copy.start())

    def next_copy(group, t, part):
        step = 1 - part
        if t:
            side = 1 if t < 0 else 0
            source = edge_out.at[group, 1 - side]
            target, arrived = edge_in.at[group, side, part], edge_sem.at[group, side, part]
        elif part:
            source, target, arrived = tile_out.at[group], rows_in.at[group, :, 2:2 + TALL], rows_sem.at[group, 1]
        else:
            source, target, arrived = tile_out.at[group, :, TALL - 2:], rows_in.at[group, :, 0:2], rows_sem.at[group, 0]
        return pltpu.make_async_remote_copy(
            src_ref=source,
            dst_ref=target,
            send_sem=next_send.at[group, t + 1, part],
            recv_sem=arrived,
            device_id=neighbour(next_section, t, step),
            device_id_type=MESH,
        )

    def all_next_copies(group, act):
        @pl.when(has_below)
        def _():
            for t in (-1, 1, 0):
                tile_when(t, lambda t=t: act(next_copy(group, t, 0)))

        for t in (-1, 1, 0):
            tile_when(t, lambda t=t: act(next_copy(group, t, 1)))

    def home_copy(group, row, remote):
        _, at_space, at_row = homes[row]
        source = tile_out.at[group, :, row]
        target = out.at[0, :, at_row, pl.ds(pl.multiple_of(tile * wide, wide), wide)]
        if not remote:
            return pltpu.make_async_copy(source, target, home_sem.at[tile, at_row])
        return pltpu.make_async_remote_copy(
            src_ref=source,
            dst_ref=target,
            send_sem=home_send.at[group, row],
            recv_sem=home_sem.at[tile, at_row],
            device_id=(section, group, at_space),
            device_id_type=MESH,
        )

    def all_home_copies(group, act):
        for row in range(TALL):
            there, at_space, _ = homes[row]
            stays = (group == tm) & (at_space == space)

            @pl.when(there & jnp.logical_not(stays))
            def _(row=row):
                act(home_copy(group, row, True))

            if act is start:
                @pl.when(there & stays)
                def _(row=row):
                    home_copy(group, row, False).start()

    def start(copy):
        copy.start()

    def wait_send(copy):
        copy.wait_send()

    def arrived(ref, sem):
        pltpu.make_async_copy(ref, ref, sem).wait()

    def activated(value):
        factor = lax.rsqrt(jnp.mean(value * value, axis=-1, keepdims=True) + 1e-06)
        value = value * factor * gain[...]
        value = 0.5 * value
        return value + value * jnp.tanh(value)

    def taps(frame, time_tap):
        summed = jnp.zeros((cells, channels), jnp.float32)
        for row_tap in range(TAPS):
            window = hidden[pl.ds(frame, frames), row_tap:row_tap + TALL]
            summed = summed + jnp.dot(
                window.reshape(cells, TAPS * channels),
                filters[TAPS * time_tap + row_tap],
                preferred_element_type=jnp.float32,
            )
        return summed

    def receive(group, part, rows):
        for side, t in ((0, -1), (1, 1)):
            tile_when(t, lambda side=side: arrived(edge_in.at[group, side, part], edge_sem.at[group, side, part]))
        arrived(rows_in.at[group, :, rows[0]:rows[1]], rows_sem.at[group, part])

    def process(group, carry):
        first = group * frames

        @pl.when(has_above)
        def _():
            receive(group, 0, (0, 2))

        @pl.when((section == 0) & has_below)
        def _():
            receive(group, 1, (2, 4))
            receive(group, 2, (4, 6))

        @pl.when(section > 0)
        def _():
            receive(group, 1, (2, 6))

        lower = lax.broadcasted_iota(jnp.int32, (edge_cells, channels), 0) >= edge_cells // 2
        pieces = []
        for side in range(2):
            above, middle, under = (
                jnp.concatenate(
                    [edge_in[group, side, p][n * edge_cells:(n + 1) * edge_cells].astype(jnp.float32)
                     for n in range(channels // LANES)],
                    axis=1,
                )
                for p in range(3)
            )
            pieces += [above, jnp.where(lower & (section == 0), under, middle)]
        halo[...] = activated(jnp.concatenate(pieces, axis=0))

        def edge_cell(side, row, frame):
            at = (2 * side * TALL + row + TALL - 2) * frames + frame
            return halo[pl.ds(at, 1), :]

        taken = TALL + 2
        given = rows_in[group].reshape(frames * taken * wide, channels).astype(jnp.float32)
        values = activated(given).reshape(frames, taken, wide, channels)
        column = lax.broadcasted_iota(jnp.int32, (wide, channels), 0)
        for frame in range(frames):
            for row in range(taken):
                here = values[frame, row]
                image_row = TALL * band + low - 1 + row
                inside_image = (image_row >= 0) & (image_row < TALL * bands)
                left = jnp.where(column == 0, edge_cell(0, row, frame), pltpu.roll(here, 1, 0))
                right = jnp.where(column == wide - 1, edge_cell(1, row, frame), pltpu.roll(here, wide - 1, 0))
                for part, shifted in enumerate((left, here, right)):
                    hidden[first + ahead + frame, row, :, part * channels:(part + 1) * channels] = (
                        jnp.where(inside_image, shifted, 0.0).astype(jnp.bfloat16)
                    )

        @pl.when(group == 0)
        def _():
            load_filters.wait()

        own = given.reshape(frames, taken, wide, channels)[:, 1:1 + TALL].reshape(cells, channels)
        summed = partial[...]
        for time_tap in range(1, TAPS):
            summed = summed + taps(first + time_tap, time_tap)
        result = own + summed
        tile_out[group] = result.astype(jnp.bfloat16).reshape(frames, TALL, wide, channels)

        @pl.when(section < sections - 1)
        def _():
            for frame in range(frames):
                for row in range(TALL):
                    source = (frame * TALL + row) * wide
                    for lane in range(channels // LANES):
                        wide_out[lane, pl.ds((row * frames + frame) * wide, wide), :] = (
                            result[source:source + wide, lane * LANES:(lane + 1) * LANES]
                        )
            for side, at in enumerate((0, wide - 1)):
                parts = [
                    wide_out[lane, pl.ds(at, edge_cells, stride=wide), :]
                    for lane in range(channels // LANES)
                ]
                edge_out[group, side] = jnp.concatenate(parts, axis=0).astype(jnp.bfloat16)
            all_next_copies(group, start)

        all_home_copies(group, start)

        @pl.when(group < groups - 1)
        def _():
            partial[...] = taps(first + frames, 0)

        return carry

    @pl.when(worker)
    def _():
        load_gain.wait()
        lax.fori_loop(0, groups, process, 0)

    for near in range(pair):
        for at in range(TILES):
            arrived(out.at[0, :, near, at * wide:(at + 1) * wide], home_sem.at[at, near])

    both_clip_copies(wait_send)

    def drain(group, carry):
        @pl.when(section < sections - 1)
        def _():
            all_next_copies(group, wait_send)

        all_home_copies(group, wait_send)
        return carry

    @pl.when(worker)
    def _():
        lax.fori_loop(0, groups, drain, 0)


def on_device(clip_features, conv_kernels, norm_gains):
    frames, pair, columns, channels = clip_features.shape
    groups = lax.axis_size("tm")
    wide = columns // TILES
    edge_cells = frames * TALL
    edge = (edge_cells * channels // LANES, LANES)
    edges = 2 * (TILES - 1)
    in_hbm = pl.BlockSpec(memory_space=pltpu.HBM)
    return pl.pallas_call(
        chain_kernel,
        out_shape=jax.ShapeDtypeStruct((1, frames, pair, columns, channels), jnp.bfloat16),
        in_specs=[in_hbm] * 3,
        out_specs=in_hbm,
        scratch_shapes=[
            pltpu.VMEM((groups, frames, TALL + 2, wide, channels), jnp.bfloat16),
            pltpu.VMEM((groups, 2, 3, *edge), jnp.bfloat16),
            pltpu.VMEM((TAPS - 1 + groups * frames, TALL + 2, wide, TAPS * channels), jnp.bfloat16),
            pltpu.VMEM((frames * TALL * wide, channels), jnp.float32),
            pltpu.VMEM((2 * 2 * edge_cells, channels), jnp.float32),
            pltpu.VMEM(conv_kernels.shape[1:], jnp.bfloat16),
            pltpu.VMEM(norm_gains.shape, jnp.float32),
            pltpu.VMEM((channels // LANES, frames * TALL * wide, LANES), jnp.float32),
            pltpu.VMEM((groups, frames, TALL, wide, channels), jnp.bfloat16),
            pltpu.VMEM((groups, 2, *edge), jnp.bfloat16),
            pltpu.VMEM((frames, pair, columns, channels), jnp.bfloat16),
            pltpu.VMEM((channels // LANES, frames * pair * columns, LANES), jnp.float32),
            pltpu.VMEM((edges, *edge), jnp.bfloat16),
            pltpu.SemaphoreType.DMA((groups, 3)),
            pltpu.SemaphoreType.DMA((groups, 2, 3)),
            pltpu.SemaphoreType.DMA((TILES, pair)),
            pltpu.SemaphoreType.DMA((2 * (edges + TILES),)),
            pltpu.SemaphoreType.DMA((groups, 3, 2)),
            pltpu.SemaphoreType.DMA((groups, TALL)),
            pltpu.SemaphoreType.DMA((3,)),
        ],
        compiler_params=pltpu.CompilerParams(
            collective_id=0, has_side_effects=True, vmem_limit_bytes=56 * 2**20
        ),
        name="chain",
    )(clip_features, conv_kernels, norm_gains)


def solution(mesh):
    return jax.shard_map(
        on_device,
        mesh=mesh,
        in_specs=(P("tm", "space", None, None), P("section", None, None, None), P("section", None)),
        out_specs=P("section", "tm", "space", None, None),
        check_vma=False,
    )
```

time: 34.8 us -> 36.2 us (1.040)
  Pallas kernels: 33.1 us -> 34.5 us
    pallas_call x1, Pallas kernels: 33.1 us -> 34.5 us  [on_device(): pl.pallas_call(chain_kernel, out_shape=jax.ShapeDtypeStruct((1, frames, p...]
where the time goes in v10:
time: 36.2 us; the launch traced here: 36 us
  Pallas kernels  34.5 us (95%)
  local copies, waits for them, and re-layouts  1.57 us (4%)
    pallas_call x1, Pallas kernels, on_device(): pl.pallas_call(chain_kernel, out_shape=jax.ShapeDtypeStruct((1, frames, p...  34.5 us
    unnamed x1, local copies, waits for them, and re-layouts  1.57 us

profile of v10, /device:TPU:27, one launch (start us, length us, event | category | flops | bytes accessed | tf_op | source)
XLA Modules:
  0.0 36.0 jit_solution(15004506468754406872)
XLA Ops:
  0.0 34.5 %chain.1 = bf16[1,2,2,64,256]{4,3,2,1,0:T(8,128)(2,1)} custom-call(bf16[2,2,64,256]{3,2,1,0:T(8,128)(2,1)} %clip.1, bf16[1,9,768,256]{3,2,1,0:T(8,128)(2,1)} %weights.1, f32[1,256]{1,0:T(1,128)} %gains.1), custom_call_target="tpu_custom_call" | custom-call | tf_op jit(solution)/shard_map/chain/pallas_call | solution.py:418
  34.5 1.6 %copy.5 = bf16[1,2,2,64,256]{4,3,2,1,0:T(8,128)(2,1)} copy(bf16[1,2,2,64,256]{4,3,2,1,0:T(8,128)(2,1)} %chain.1) | data formatting | bytes 262144

commit v11 on v8

--- a/solution.py
+++ b/solution.py
@@ -469,7 +469,7 @@
             pltpu.SemaphoreType.DMA((3,)),
         ],
         compiler_params=pltpu.CompilerParams(
-            collective_id=0, has_side_effects=True, vmem_limit_bytes=56 * 2**20
+            collective_id=0, has_side_effects=True, vmem_limit_bytes=55040 * 2**10
         ),
         name="chain",
     )(clip_features, conv_kernels, norm_gains)

time: 31.6 us -> 31.4 us (level)
    unnamed x1 -> x3, local copies, waits for them, and re-layouts: 1.57 us -> 1.34 us
where the time goes in v11:
time: 31.4 us; the launch traced here: 31.3 us
  Pallas kernels  29.9 us (95%)
  local copies, waits for them, and re-layouts  1.34 us (4%)
    pallas_call x1, Pallas kernels, on_device(): pl.pallas_call(chain_kernel, out_shape=jax.ShapeDtypeStruct((1, frames, p...  29.9 us
    unnamed x3, local copies, waits for them, and re-layouts  1.34 us

profile of v11, /device:TPU:123, one launch (start us, length us, event | category | flops | bytes accessed | tf_op | source)
XLA Modules:
  0.0 31.3 jit_solution(11505226669828040881)
XLA Ops:
  0.0 0.0 copy-start
  0.0 0.7 %copy-done = f32[1,256]{1,0:T(1,128)S(1)} copy-done((f32[1,256]{1,0:T(1,128)S(1)}, f32[1,256]{1,0:T(1,128)}, u32[]{:S(2)}) %copy-start) | copy-done | bytes 1048
  0.7 29.9 %chain.1 = bf16[1,2,2,64,256]{4,3,2,1,0:T(8,128)(2,1)S(1)} custom-call(bf16[2,2,64,256]{3,2,1,0:T(8,128)(2,1)} %clip.1, bf16[1,9,768,256]{3,2,1,0:T(8,128)(2,1)} %weights.1, f32[1,256]{1,0:T(1,128)S(1)} %copy-done), custom_call_target="tpu_custom_call" | custom-call | tf_op jit(solution)/shard_map/chain/pallas_call | solution.py:437
  30.6 0.7 %copy.5 = bf16[1,2,2,64,256]{4,3,2,1,0:T(8,128)(2,1)} copy(bf16[1,2,2,64,256]{4,3,2,1,0:T(8,128)(2,1)S(1)} %chain.1) | data formatting | bytes 262144
Async XLA Ops:
  0.0 0.7 %copy-start = (f32[1,256]{1,0:T(1,128)S(1)}, f32[1,256]{1,0:T(1,128)}, u32[]{:S(2)}) copy-start(f32[1,256]{1,0:T(1,128)} %gains.1) | copy-start | bytes 3076

commit v12 on v11

--- a/solution.py
+++ b/solution.py
@@ -11,6 +11,7 @@
 TALL = 4
 TILES = 4
 LANES = 128
+SOURCES = (0, 3, 1, 2)
 
 
 def chain_kernel(
@@ -30,7 +31,7 @@
     run = tm // 2
     tile = 2 * half + run
     worker = tm % 2 == WORKER
-    sender = section == tm % sections
+    sender = section == sum(jnp.where(tm == group, source, 0) for group, source in enumerate(SOURCES))
     frames, pair, columns, channels = clip.shape
     wide = columns // TILES
     cells = frames * TALL * wide
@@ -74,19 +75,19 @@
 
     @pl.when(worker & (section == 0))
     def _():
-        for group in range(groups):
+        for group, source in enumerate(SOURCES):
             for near in range(2):
-                greet((group % sections, group, 2 * band + near))
+                greet((source, group, 2 * band + near))
 
         @pl.when(band > 0)
         def _():
-            for group in range(groups):
-                greet((group % sections, group, jnp.maximum(2 * band - 1, 0)))
+            for group, source in enumerate(SOURCES):
+                greet((source, group, jnp.maximum(2 * band - 1, 0)))
 
         @pl.when(band < bands - 1)
         def _():
-            for group in range(groups):
-                greet((group % sections, group, jnp.minimum(2 * band + 2, 2 * bands - 1)))
+            for group, source in enumerate(SOURCES):
+                greet((source, group, jnp.minimum(2 * band + 2, 2 * bands - 1)))
 
     load_filters = pltpu.make_async_copy(weights.at[0], filters, load_sem.at[0])
     load_gain = pltpu.make_async_copy(gains, gain, load_sem.at[1])

time: 31.4 us -> 31.6 us (level)
  the two profiles are of different devices: /device:TPU:123 before, /device:TPU:159 now
where the time goes in v12:
time: 31.6 us; the launch traced here: 31.4 us
  Pallas kernels  30.1 us (95%)
  local copies, waits for them, and re-layouts  1.34 us (4%)
    pallas_call x1, Pallas kernels, on_device(): pl.pallas_call(chain_kernel, out_shape=jax.ShapeDtypeStruct((1, frames, p...  30.1 us
    unnamed x3, local copies, waits for them, and re-layouts  1.34 us

profile of v12, /device:TPU:159, one launch (start us, length us, event | category | flops | bytes accessed | tf_op | source)
XLA Modules:
  0.0 31.4 jit_solution(8294158642416290952)
XLA Ops:
  0.0 0.0 copy-start
  0.0 0.7 %copy-done = f32[1,256]{1,0:T(1,128)S(1)} copy-done((f32[1,256]{1,0:T(1,128)S(1)}, f32[1,256]{1,0:T(1,128)}, u32[]{:S(2)}) %copy-start) | copy-done | bytes 1048
  0.7 30.1 %chain.1 = bf16[1,2,2,64,256]{4,3,2,1,0:T(8,128)(2,1)S(1)} custom-call(bf16[2,2,64,256]{3,2,1,0:T(8,128)(2,1)} %clip.1, bf16[1,9,768,256]{3,2,1,0:T(8,128)(2,1)} %weights.1, f32[1,256]{1,0:T(1,128)S(1)} %copy-done), custom_call_target="tpu_custom_call" | custom-call | tf_op jit(solution)/shard_map/chain/pallas_call | solution.py:438
  30.8 0.7 %copy.5 = bf16[1,2,2,64,256]{4,3,2,1,0:T(8,128)(2,1)} copy(bf16[1,2,2,64,256]{4,3,2,1,0:T(8,128)(2,1)S(1)} %chain.1) | data formatting | bytes 262144
Async XLA Ops:
  0.0 0.7 %copy-start = (f32[1,256]{1,0:T(1,128)S(1)}, f32[1,256]{1,0:T(1,128)}, u32[]{:S(2)}) copy-start(f32[1,256]{1,0:T(1,128)} %gains.1) | copy-start | bytes 3076

commit v13 on v11

--- a/solution.py
+++ b/solution.py
@@ -30,7 +30,7 @@
     run = tm // 2
     tile = 2 * half + run
     worker = tm % 2 == WORKER
-    sender = section == tm % sections
+    sender = section == jnp.where((tm == 0) & (space == 0), 1, tm % sections)
     frames, pair, columns, channels = clip.shape
     wide = columns // TILES
     cells = frames * TALL * wide
@@ -76,7 +76,8 @@
     def _():
         for group in range(groups):
             for near in range(2):
-                greet((group % sections, group, 2 * band + near))
+                source = jnp.where(band == 0, 1, 0) if group + near == 0 else group % sections
+                greet((source, group, 2 * band + near))
 
         @pl.when(band > 0)
         def _():

time: 31.4 us -> 31.3 us (level)
  no operation moved by 1% of the time
where the time goes in v13:
time: 31.3 us; the launch traced here: 31.2 us
  Pallas kernels  29.8 us (95%)
  local copies, waits for them, and re-layouts  1.34 us (4%)
    pallas_call x1, Pallas kernels, on_device(): pl.pallas_call(chain_kernel, out_shape=jax.ShapeDtypeStruct((1, frames, p...  29.8 us
    unnamed x3, local copies, waits for them, and re-layouts  1.34 us

profile of v13, /device:TPU:123, one launch (start us, length us, event | category | flops | bytes accessed | tf_op | source)
XLA Modules:
  0.0 31.2 jit_solution(5752645867834412419)
XLA Ops:
  0.0 0.0 copy-start
  0.0 0.7 %copy-done = f32[1,256]{1,0:T(1,128)S(1)} copy-done((f32[1,256]{1,0:T(1,128)S(1)}, f32[1,256]{1,0:T(1,128)}, u32[]{:S(2)}) %copy-start) | copy-done | bytes 1048
  0.7 29.8 %chain.1 = bf16[1,2,2,64,256]{4,3,2,1,0:T(8,128)(2,1)S(1)} custom-call(bf16[2,2,64,256]{3,2,1,0:T(8,128)(2,1)} %clip.1, bf16[1,9,768,256]{3,2,1,0:T(8,128)(2,1)} %weights.1, f32[1,256]{1,0:T(1,128)S(1)} %copy-done), custom_call_target="tpu_custom_call" | custom-call | tf_op jit(solution)/shard_map/chain/pallas_call | solution.py:438
  30.5 0.7 %copy.5 = bf16[1,2,2,64,256]{4,3,2,1,0:T(8,128)(2,1)} copy(bf16[1,2,2,64,256]{4,3,2,1,0:T(8,128)(2,1)S(1)} %chain.1) | data formatting | bytes 262144
Async XLA Ops:
  0.0 0.7 %copy-start = (f32[1,256]{1,0:T(1,128)S(1)}, f32[1,256]{1,0:T(1,128)}, u32[]{:S(2)}) copy-start(f32[1,256]{1,0:T(1,128)} %gains.1) | copy-start | bytes 3076

commit v14 on v11

--- a/solution.py
+++ b/solution.py
@@ -274,6 +274,18 @@
             )
         return summed
 
+    def send_home(group):
+        for near in range(2):
+            own_home = (group == tm) & (near == half)
+
+            @pl.when(own_home)
+            def _(near=near):
+                own_copy(group, near).start()
+
+            @pl.when(jnp.logical_not(own_home))
+            def _(near=near):
+                home_copy(group, near).start()
+
     def process(group, carry):
         first = group * frames
 
@@ -377,16 +389,9 @@
             for condition, copy in next_copies(group):
                 when(condition, copy.start)
 
-        for near in range(2):
-            own_home = (group == tm) & (near == half)
-
-            @pl.when(own_home)
-            def _(near=near):
-                own_copy(group, near).start()
-
-            @pl.when(jnp.logical_not(own_home))
-            def _(near=near):
-                home_copy(group, near).start()
+        @pl.when(section == sections - 1)
+        def _():
+            send_home(group)
 
         @pl.when(group < groups - 1)
         def _():
@@ -398,6 +403,10 @@
     def _():
         load_gain.wait()
         lax.fori_loop(0, groups, process, 0)
+
+        @pl.when(section < sections - 1)
+        def _():
+            lax.fori_loop(0, groups, lambda group, carry: (send_home(group), carry)[1], 0)
 
     for at in range(TILES):
         arrived(out.at[0, :, :, at * wide:(at + 1) * wide], home_sem.at[at])

time: 31.4 us -> 31.3 us (level)
  no operation moved by 1% of the time
where the time goes in v14:
time: 31.3 us; the launch traced here: 31.2 us
  Pallas kernels  29.9 us (96%)
  local copies, waits for them, and re-layouts  1.34 us (4%)
    pallas_call x1, Pallas kernels, on_device(): pl.pallas_call(chain_kernel, out_shape=jax.ShapeDtypeStruct((1, frames, p...  29.9 us
    unnamed x3, local copies, waits for them, and re-layouts  1.34 us

profile of v14, /device:TPU:123, one launch (start us, length us, event | category | flops | bytes accessed | tf_op | source)
XLA Modules:
  0.0 31.2 jit_solution(4550295452615620298)
XLA Ops:
  0.0 0.0 copy-start
  0.0 0.7 %copy-done = f32[1,256]{1,0:T(1,128)S(1)} copy-done((f32[1,256]{1,0:T(1,128)S(1)}, f32[1,256]{1,0:T(1,128)}, u32[]{:S(2)}) %copy-start) | copy-done | bytes 1048
  0.7 29.9 %chain.1 = bf16[1,2,2,64,256]{4,3,2,1,0:T(8,128)(2,1)S(1)} custom-call(bf16[2,2,64,256]{3,2,1,0:T(8,128)(2,1)} %clip.1, bf16[1,9,768,256]{3,2,1,0:T(8,128)(2,1)} %weights.1, f32[1,256]{1,0:T(1,128)S(1)} %copy-done), custom_call_target="tpu_custom_call" | custom-call | tf_op jit(solution)/shard_map/chain/pallas_call | solution.py:446
  30.5 0.7 %copy.5 = bf16[1,2,2,64,256]{4,3,2,1,0:T(8,128)(2,1)} copy(bf16[1,2,2,64,256]{4,3,2,1,0:T(8,128)(2,1)S(1)} %chain.1) | data formatting | bytes 262144
Async XLA Ops:
  0.0 0.7 %copy-start = (f32[1,256]{1,0:T(1,128)S(1)}, f32[1,256]{1,0:T(1,128)}, u32[]{:S(2)}) copy-start(f32[1,256]{1,0:T(1,128)} %gains.1) | copy-start | bytes 3076

commit v15 on v11

--- a/solution.py
+++ b/solution.py
@@ -101,7 +101,7 @@
         load_gain.start()
         load_filters.start()
 
-    steps = [(t, b) for t in (-1, 1, 0) for b in (-1, 1, 0)]
+    steps = [(t, b) for b in (-1, 0, 1) for t in (-1, 1, 0)]
 
     @pl.when(worker & (section > 0))
     def _():

time: 31.4 us -> 31.3 us (level)
  no operation moved by 1% of the time
where the time goes in v15:
time: 31.3 us; the launch traced here: 31.2 us
  Pallas kernels  29.8 us (95%)
  local copies, waits for them, and re-layouts  1.34 us (4%)
    pallas_call x1, Pallas kernels, on_device(): pl.pallas_call(chain_kernel, out_shape=jax.ShapeDtypeStruct((1, frames, p...  29.8 us
    unnamed x3, local copies, waits for them, and re-layouts  1.34 us

profile of v15, /device:TPU:123, one launch (start us, length us, event | category | flops | bytes accessed | tf_op | source)
XLA Modules:
  0.0 31.2 jit_solution(11687977643018113971)
XLA Ops:
  0.0 0.0 copy-start
  0.0 0.7 %copy-done = f32[1,256]{1,0:T(1,128)S(1)} copy-done((f32[1,256]{1,0:T(1,128)S(1)}, f32[1,256]{1,0:T(1,128)}, u32[]{:S(2)}) %copy-start) | copy-done | bytes 1048
  0.7 29.8 %chain.1 = bf16[1,2,2,64,256]{4,3,2,1,0:T(8,128)(2,1)S(1)} custom-call(bf16[2,2,64,256]{3,2,1,0:T(8,128)(2,1)} %clip.1, bf16[1,9,768,256]{3,2,1,0:T(8,128)(2,1)} %weights.1, f32[1,256]{1,0:T(1,128)S(1)} %copy-done), custom_call_target="tpu_custom_call" | custom-call | tf_op jit(solution)/shard_map/chain/pallas_call | solution.py:437
  30.5 0.7 %copy.5 = bf16[1,2,2,64,256]{4,3,2,1,0:T(8,128)(2,1)} copy(bf16[1,2,2,64,256]{4,3,2,1,0:T(8,128)(2,1)S(1)} %chain.1) | data formatting | bytes 262144
Async XLA Ops:
  0.0 0.7 %copy-start = (f32[1,256]{1,0:T(1,128)S(1)}, f32[1,256]{1,0:T(1,128)}, u32[]{:S(2)}) copy-start(f32[1,256]{1,0:T(1,128)} %gains.1) | copy-start | bytes 3076
